TPU v7x, 32 devices: a whole 2x2x4 slice. The times are simulated.
32 devices in a mesh: section: 4 (over x, core), head: 4 (over z), kv: 2 (over y).
Axes of the slice: x: 2, y: 2, z: 4, core: 2. Of those that a mesh axis runs over, the one named last changes fastest.
Arguments:
- tokens: bfloat16 [4, 256, 4096], P('section', 'kv', 'head'), may hold values from -40 to 40
- w_query: bfloat16 [4096, 4096], P(('section', 'kv'), 'head'), may hold values from -0.21875 to 0.21875
- w_keyvalue: bfloat16 [4096, 2, 4096], P(('section', 'kv'), None, 'head'), may hold values from -0.09375 to 0.09375
- cache_keys: bfloat16 [4, 4096, 4096], P('section', 'kv', 'head'), may hold values from -800 to 800
- cache_values: bfloat16 [4, 4096, 4096], P('section', 'kv', 'head'), may hold values from -6 to 6
- key_start: int32 [4], P('section'), may hold values from 0 to 2047
- key_end: int32 [4], P('section'), may hold values from 3072 to 4096
- w_out: bfloat16 [4096, 4096], P('head', ('section', 'kv')), may hold values from -0.375 to 0.375
Outputs:
- attention_out: bfloat16 [4, 256, 4096], P('section', 'kv', 'head')
All inputs are finite; a program needn't handle non-finite values.
Results may differ from a plain program's by a relative error of at most 0.014.
The roundings to bfloat16 on the way count: a program that leaves them out, or rounds other values in their place, can miss the bound.
Values may be sent and summed in bfloat16 or wider, within the bound.
A program may use at most 128 MiB of HBM per device.

v0:
```python
import jax
import jax.numpy as jnp
from jax import lax
from jax.sharding import PartitionSpec as P

HD = 128


def add_projection(pieces, inputs):
    query_rows = jnp.dot(inputs, pieces[0], preferred_element_type=jnp.float32)
    pair_weight = pieces[1].reshape(pieces[1].shape[0], -1)
    pair_rows = jnp.dot(inputs, pair_weight, preferred_element_type=jnp.float32)
    return (query_rows, pair_rows)


def shards(tokens, w_query, w_keyvalue, cache_keys, cache_values, key_start, key_end, w_out):
    local_rows = tokens.shape[1]
    head_width = tokens.shape[2]
    heads_here = head_width // HD
    gathered = lax.all_gather(tokens, "head", axis=2, tiled=True)[0]
    widened = gathered.astype(jnp.float32)
    scaled = widened * lax.rsqrt(jnp.mean(widened * widened, axis=1, keepdims=True) + 1e-05)
    normed = scaled.astype(jnp.bfloat16)
    query_sum, pair_sum = add_projection(
        (
            lax.all_gather(w_query, ("section", "kv"), axis=0, tiled=True),
            lax.all_gather(w_keyvalue, ("section", "kv"), axis=0, tiled=True),
        ),
        normed,
    )
    queries_own = query_sum.astype(jnp.bfloat16)
    new_keys = pair_sum[:, :head_width].astype(jnp.bfloat16)
    new_values = pair_sum[:, head_width:].astype(jnp.bfloat16)
    queries = lax.all_gather(queries_own, "kv", axis=0, tiled=True)
    total_rows = queries.shape[0]
    kv_index = lax.axis_index("kv")
    cache_rows = cache_keys.shape[1]
    keys_all = jnp.concatenate([cache_keys[0], new_keys], axis=0).reshape(-1, heads_here, HD)
    values_all = jnp.concatenate([cache_values[0], new_values], axis=0).reshape(-1, heads_here, HD)
    cache_place = kv_index * cache_rows + lax.iota(jnp.int32, cache_rows)
    cache_usable = (cache_place >= key_start[0]) & (cache_place < key_end[0])
    new_place = kv_index * local_rows + lax.iota(jnp.int32, local_rows)
    block_rows = 512 if total_rows % 512 == 0 else total_rows
    count_blocks = total_rows // block_rows
    grouped = queries.reshape(count_blocks, block_rows, heads_here, HD)
    score_scale = HD ** (-0.5)

    def attend(packed):
        query_block, block_index = packed
        query_place = block_index * block_rows + lax.iota(jnp.int32, block_rows)
        scores = (
            jnp.einsum("qhd,khd->hqk", query_block, keys_all, preferred_element_type=jnp.float32)
            * score_scale
        )
        usable = jnp.concatenate(
            [
                jnp.broadcast_to(cache_usable[None, :], (block_rows, cache_rows)),
                new_place[None, :] <= query_place[:, None],
            ],
            axis=1,
        )
        masked = jnp.where(usable[None], scores, -1e30)
        row_peak = jnp.max(masked, axis=2)
        weights = jnp.where(usable[None], jnp.exp(masked - row_peak[:, :, None]), 0.0).astype(
            jnp.bfloat16
        )
        row_total = jnp.sum(weights.astype(jnp.float32), axis=2)
        mixture = jnp.einsum(
            "hqk,khd->qhd", weights, values_all, preferred_element_type=jnp.float32
        )
        return (row_peak.T, row_total.T, mixture.reshape(block_rows, head_width))

    peaks, totals, mixtures = lax.map(attend, (grouped, jnp.arange(count_blocks, dtype=jnp.int32)))
    peaks = peaks.reshape(total_rows, heads_here)
    totals = totals.reshape(total_rows, heads_here)
    mixtures = mixtures.reshape(total_rows, head_width)
    gathered_peaks, gathered_totals, gathered_mixtures = (
        lax.all_to_all(peaks[None], "kv", split_axis=1, concat_axis=0, tiled=True),
        lax.all_to_all(totals[None], "kv", split_axis=1, concat_axis=0, tiled=True),
        lax.all_to_all(mixtures[None], "kv", split_axis=1, concat_axis=0, tiled=True),
    )
    highest = jnp.max(gathered_peaks, axis=0)
    factors = jnp.exp(gathered_peaks - highest[None])
    own_total = jnp.sum(gathered_totals * factors, axis=0)
    split_mixture = gathered_mixtures.reshape(
        gathered_mixtures.shape[0], local_rows, heads_here, HD
    )
    own_mixture = jnp.sum(split_mixture * factors[..., None], axis=0).reshape(
        local_rows, head_width
    )
    attended = (
        (own_mixture.reshape(local_rows, heads_here, HD) / own_total[..., None])
        .reshape(local_rows, head_width)
        .astype(jnp.bfloat16)
    )
    terms = jnp.dot(
        attended,
        lax.all_gather(w_out, ("section", "kv"), axis=1, tiled=True),
        preferred_element_type=jnp.float32,
    )
    summed = lax.psum_scatter(terms, "head", scatter_dimension=1, tiled=True)
    return summed.astype(jnp.bfloat16)[None]


def solution(mesh):
    placed = (
        P("section", "kv", "head"),
        P(("section", "kv"), "head"),
        P(("section", "kv"), None, "head"),
        P("section", "kv", "head"),
        P("section", "kv", "head"),
        P("section"),
        P("section"),
        P("head", ("section", "kv")),
    )
    return jax.shard_map(
        shards, mesh=mesh, in_specs=placed, out_specs=P("section", "kv", "head"), check_vma=False
    )
```

profile of v0, /device:TPU:28, one launch (start us, length us, event | category | flops | bytes accessed | tf_op | source)
XLA Modules:
  0.0 323.9 jit_solution(10903369259724592871)
XLA Ops:
  6.5 0.7 all-gather.5.cloned.1.call-update
  7.3 0.0 all-gather.9.cloned.1.call-start
  7.3 0.7 all-gather.9.cloned.1.call-update
  8.0 0.0 all-gather.7.cloned.1.call-start
  8.1 0.7 all-gather.7.cloned.1.call-update
  8.7 0.0 all-gather.11.cloned.1.call-start
  8.8 0.5 all-gather.11.cloned.1.call-update
  10.6 6.5 %copy.35 = bf16[1,2048,1024]{1,2,0:T(8,128)(2,1)} copy(bf16[1,2048,1024]{2,1,0:T(8,128)(2,1)} %param.11) | data formatting | bytes 8388608 | tf_op args[3]
  17.1 6.5 %copy.36 = bf16[2048,8,128]{2,0,1:T(8,128)(2,1)} copy(bf16[2048,8,128]{0,2,1:T(8,128)(2,1)} %bitcast.69) | data formatting | bytes 8388608 | tf_op jit(solution)/shard_map/concatenate | solution.py:38
  23.7 0.1 pad_add_fusion
  23.8 12.6 %all-gather.5.cloned.1.call-done = bf16[1,128,4096]{2,1,0:T(8,128)(2,1)} async-done(((bf16[1,128,1024]{2,1,0:T(8,128)(2,1)}), bf16[1,128,4096]{2,1,0:T(8,128)(2,1)}) %all-gather.5.cloned.1.call-update) | async-done | bytes 1048592 | tf_op jit(solution)/shard_map/all_gather | solution.py:20
  36.4 1.5 fusion.11
  37.9 55.4 %all-gather.9.cloned.1.call-done = bf16[4096,1024]{1,0:T(8,128)(2,1)} async-done(((bf16[512,1024]{1,0:T(8,128)(2,1)}), bf16[4096,1024]{1,0:T(8,128)(2,1)}) %all-gather.9.cloned.1.call-update) | async-done | bytes 8388624 | tf_op jit(solution)/shard_map/all_gather | solution.py:26
  93.3 5.0 %convolution_convert_fusion.1 = bf16[128,1024]{1,0:T(8,128)(2,1)S(1)} fusion(bf16[4096,1024]{1,0:T(8,128)(2,1)} %all-gather.9.cloned.1.call-done, bf16[1,128,4096]{2,1,0:T(8,128)(2,1)} %all-gather.5.cloned.1.call-done, f32[128]{0:T(128)S(1)} %add_rsqrt_fusion), kind=kOutput, calls=%fused_computation.21 | convolution fusion | flops 1075445760 | bytes 9699840 | tf_op jit(solution)/shard_map/dot_general | solution.py:10
  98.3 10.2 %all_gather.18 = bf16[256,1024]{1,0:T(8,128)(2,1)S(1)} all-gather(bf16[128,1024]{1,0:T(8,128)(2,1)S(1)} %convolution_convert_fusion.1), channel_id=1, replica_groups=mesh['section'=4,'head'=4,'kv'=2] {'kv'}, dimensions={0}, use_global_device_ids=true | all-gather | bytes 786432 | tf_op jit(solution)/shard_map/all_gather | solution.py:34
  108.5 76.2 %all-gather.7.cloned.1.call-done = bf16[4096,2,1024]{2,1,0:T(2,128)(2,1)} async-done(((bf16[512,2,1024]{2,1,0:T(2,128)(2,1)}), bf16[4096,2,1024]{2,1,0:T(2,128)(2,1)}) %all-gather.7.cloned.1.call-update) | async-done | bytes 16777232 | tf_op jit(solution)/shard_map/all_gather | solution.py:27
  184.7 12.1 %copy.50 = bf16[512,8,2,1024]{3,1,2,0:T(8,128)(2,1)S(1)} copy(bf16[512,8,2,1024]{3,2,1,0:T(2,128)(2,1)} %bitcast.68) | data formatting | bytes 33554432
  196.8 2.5 convolution_convert_fusion
  199.5 8.1 %fusion = (f32[8,256]{1,0:T(8,128)S(1)}, f32[8,256,2176]{2,1,0:T(8,128)}) fusion(pred[256,2176]{1,0:T(8,128)(4,1)S(1)} %pad_add_fusion, bf16[128,8,128]{2,0,1:T(8,128)(2,1)S(1)} %bitcast.79, bf16[2048,8,128]{2,0,1:T(8,128)(2,1)S(1)} %copy-done.1, bf16[256,1024]{1,0:T(8,128)(2,1)S(1)} %all_gather.18), kind=kOutput, calls=%fused_computation.3 | convolution fusion | flops 1163130880 | bytes 23371776 | tf_op jit(solution)/shard_map/while/body/eval_jaxpr/qhd,khd->hqk/dot_general | solution.py:52
  207.6 8.8 %convert_reduce_fusion = f32[8,256]{1,0:T(8,128)S(1)} fusion(f32[8,256]{1,0:T(8,128)S(1)} %get-tuple-element.25, f32[8,256,2176]{2,1,0:T(8,128)} %get-tuple-element.26, pred[256,2176]{1,0:T(8,128)(4,1)S(1)} %pad_add_fusion), kind=kLoop, calls=%fused_computation | loop fusion | flops 31193088 | bytes 18399232 | tf_op jit(solution)/shard_map/while/body/eval_jaxpr/reduce_sum | solution.py:67
  216.4 0.1 copy.45
  216.5 0.5 broadcast.61
  217.0 0.9 reduce.1
  217.9 0.7 reshape.100
  218.6 4.6 %all-to-all-start.2 = ((f32[2,1,1024]{2,1,0:T(1,128)}), f32[2,1,1024]{2,1,0:T(1,128)S(1)}, u32[]{:S(2)}, u32[]{:S(2)}) async-start(f32[2,1,1024]{2,1,0:T(1,128)} %reshape.100), calls=%async_computation.2 | async-start | bytes 16384 | tf_op jit(solution)/shard_map/all_to_all | solution.py:79
  223.2 6.5 %copy.33 = bf16[1,2048,1024]{1,2,0:T(8,128)(2,1)} copy(bf16[1,2048,1024]{2,1,0:T(8,128)(2,1)} %param.12) | data formatting | bytes 8388608 | tf_op args[4]
  229.7 0.2 copy.47
  229.9 0.1 copy.40
  230.0 0.9 reduce.3
  230.9 0.7 reshape.98
  231.7 3.4 %all-to-all-start.1 = ((f32[2,1,1024]{2,1,0:T(1,128)}), f32[2,1,1024]{2,1,0:T(1,128)S(1)}, u32[]{:S(2)}, u32[]{:S(2)}) async-start(f32[2,1,1024]{2,1,0:T(1,128)} %reshape.98), calls=%async_computation.1 | async-start | bytes 16384 | tf_op jit(solution)/shard_map/all_to_all | solution.py:78
  235.0 10.3 %fusion.1 = f32[8,128,256]{2,1,0:T(8,128)S(1)} fusion(bf16[128,8,128]{0,2,1:T(8,128)(2,1)S(1)} %bitcast.78, bf16[2048,8,128]{0,2,1:T(8,128)(2,1)} %bitcast.70, f32[8,256,2176]{2,1,0:T(8,128)} %get-tuple-element.26, f32[8,256]{1,0:T(8,128)S(1)} %get-tuple-element.25, pred[256,2176]{1,0:T(8,128)(4,1)S(1)} %pad_add_fusion), kind=kOutput, calls=%fused_computation.4 | convolution fusion | flops 1172045824 | bytes 23896064 | tf_op jit(solution)/shard_map/while/body/eval_jaxpr/hqk,khd->qhd/dot_general | solution.py:68
  245.4 1.9 copy.39
  247.3 3.6 %all-to-all-start = ((f32[1,256,1024]{2,0,1:T(1,128)}), f32[1,256,1024]{2,0,1:T(1,128)S(1)}, u32[]{:S(2)}, u32[]{:S(2)}) async-start(f32[1,256,1024]{2,0,1:T(1,128)} %copy.39), calls=%async_computation | async-start | bytes 2097152 | tf_op jit(solution)/shard_map/all_to_all | solution.py:80
  250.9 0.0 reduce-scatter.2.cloned.1.call-start
  250.9 0.6 reduce.2
  251.5 0.2 reshape.101
  251.8 0.1 copy.46
  251.9 0.6 reduce.4
  252.5 0.2 reshape.99
  252.7 0.1 copy.42
  252.9 10.6 %all-to-all-done = f32[1,256,1024]{2,0,1:T(1,128)S(1)} async-done(((f32[1,256,1024]{2,0,1:T(1,128)}), f32[1,256,1024]{2,0,1:T(1,128)S(1)}, u32[]{:S(2)}, u32[]{:S(2)}) %all-to-all-start) | async-done | bytes 1048608 | tf_op jit(solution)/shard_map/all_to_all | solution.py:80
  263.5 1.0 copy.44
  264.5 1.5 fusion.17
  266.0 0.1 fusion.22
  266.0 6.0 %fusion.28 = f32[128,4096]{1,0:T(8,128)} fusion(bf16[128,1024]{0,1:T(8,128)(2,1)S(1)} %fusion.22, bf16[1024,4096]{1,0:T(8,128)(2,1)} %all-gather.11.cloned.1.call-done), kind=kOutput, calls=%fused_computation.45 | convolution fusion | flops 1073741824 | bytes 10747904 | tf_op jit(solution)/shard_map/dot_general | solution.py:96
  272.1 43.5 %reduce-scatter.2.cloned.1.call-done = f32[128,1024]{1,0:T(8,128)} async-done(((f32[128,4096]{1,0:T(8,128)}), f32[128,1024]{1,0:T(8,128)}) %reduce-scatter.2.cloned.1.call-update) | async-done | bytes 524304 | tf_op jit(solution)/shard_map/reduce_scatter | solution.py:101
  315.6 1.8 convert_bitcast_fusion.1
  (20 shorter events, 0.3 us)
Async XLA Ops:
  6.5 29.9 %all-gather.5.cloned.1.call-start = ((), (), s32[]{:S(2)}) async-start(), calls=%async_computation.4 | async-start | bytes 1310720 | tf_op jit(solution)/shard_map/all_gather | solution.py:20
  7.3 86.0 %all-gather.9.cloned.1.call-start = ((), (), s32[]{:S(2)}) async-start(), calls=%async_computation.6 | async-start | bytes 9437184 | tf_op jit(solution)/shard_map/all_gather | solution.py:26
  8.0 176.7 %all-gather.7.cloned.1.call-start = ((), (), s32[]{:S(2)}) async-start(), calls=%async_computation.5 | async-start | bytes 18874368 | tf_op jit(solution)/shard_map/all_gather | solution.py:27
  8.7 257.3 %all-gather.11.cloned.1.call-start = ((), (), s32[]{:S(2)}) async-start(), calls=%async_computation.7 | async-start | bytes 9437184 | tf_op jit(solution)/shard_map/all_gather | solution.py:98
  184.7 12.1 %copy-start = (bf16[1,128,4096]{2,1,0:T(8,128)(2,1)S(1)}, bf16[1,128,4096]{2,1,0:T(8,128)(2,1)}, u32[]{:S(2)}) copy-start(bf16[1,128,4096]{2,1,0:T(8,128)(2,1)} %all-gather.5.cloned.1.call-done) | copy-start | bytes 3145732
  196.8 2.7 copy-start.1
  218.6 13.0 %all-to-all-start.2 = ((f32[2,1,1024]{2,1,0:T(1,128)}), f32[2,1,1024]{2,1,0:T(1,128)S(1)}, u32[]{:S(2)}, u32[]{:S(2)}) async-start(f32[2,1,1024]{2,1,0:T(1,128)} %reshape.100), calls=%async_computation.2 | async-start | bytes 16384 | tf_op jit(solution)/shard_map/all_to_all | solution.py:79
  231.7 15.7 %all-to-all-start.1 = ((f32[2,1,1024]{2,1,0:T(1,128)}), f32[2,1,1024]{2,1,0:T(1,128)S(1)}, u32[]{:S(2)}, u32[]{:S(2)}) async-start(f32[2,1,1024]{2,1,0:T(1,128)} %reshape.98), calls=%async_computation.1 | async-start | bytes 16384 | tf_op jit(solution)/shard_map/all_to_all | solution.py:78
  247.3 16.2 %all-to-all-start = ((f32[1,256,1024]{2,0,1:T(1,128)}), f32[1,256,1024]{2,0,1:T(1,128)S(1)}, u32[]{:S(2)}, u32[]{:S(2)}) async-start(f32[1,256,1024]{2,0,1:T(1,128)} %copy.39), calls=%async_computation | async-start | bytes 2097152 | tf_op jit(solution)/shard_map/all_to_all | solution.py:80
  250.9 64.7 %reduce-scatter.2.cloned.1.call-start = ((), (), s32[]{:S(2)}) async-start(), calls=%async_computation.8 | async-start | bytes 2621440 | tf_op jit(solution)/shard_map/reduce_scatter | solution.py:101
Sparse Core Ops, SparseCore 0:
  8.9 27.4 all-gather.4
  38.3 54.9 all-gather.8
  95.2 89.4 all-gather.6
  186.4 55.9 all-gather.10
  272.2 43.3 reduce-scatter.1
where the time goes:
time: 328 us; the launch traced here: 324 us
  waiting for transfers between devices  201 us (61%)
  local copies, waits for them, and re-layouts  37.7 us (11%)
  matrix products  32 us (10%)
  other arithmetic  16.8 us (5%)
  between operations  14.7 us (4%)
  starting transfers between devices  11.7 us (4%)
  blocking collectives  10.2 us (3%)
    all_gather x1, waiting for transfers between devices, shards(): lax.all_gather(w_keyvalue, ('section', 'kv'), axis=0, tiled=True)  76.2 us
    all_gather x1, waiting for transfers between devices, shards(): lax.all_gather(w_query, ('section', 'kv'), axis=0, tiled=True)  55.4 us
    reduce_scatter x1, waiting for transfers between devices, shards(): summed = lax.psum_scatter(terms, 'head', scatter_dimension=1, tiled=True)  43.5 us
    unnamed x13, local copies, waits for them, and re-layouts  27.6 us
    all_gather x1, waiting for transfers between devices, shards(): gathered = lax.all_gather(tokens, 'head', axis=2, tiled=True)[0]  12.6 us
    all_to_all x1, waiting for transfers between devices, shards(): lax.all_to_all(mixtures[None], 'kv', split_axis=1, concat_axis=0, tiled=T...  10.6 us
    dot_general x1, matrix products, attend(): jnp.einsum('hqk,khd->qhd', weights, values_all, preferred_element_type=jn...  10.3 us
    all_gather x1, blocking collectives, shards(): queries = lax.all_gather(queries_own, 'kv', axis=0, tiled=True)  10.2 us
  transfers between devices with their start and end apart: 8, of which 5 were waited for; matrix products, arithmetic and copies ran while one was open for 24% of the time, Pallas kernels for 0%

commit v1 on v0

v1 whole, which is shorter than its diff:
```python
import functools
import math

import jax
import jax.numpy as jnp
from jax import lax
from jax.experimental import pallas as pl
from jax.experimental.pallas import tpu as pltpu
from jax.sharding import PartitionSpec as P

HD = 128
MESH = pl.DeviceIdType.MESH
LOW = -1e30
FLOOR = -1e29
RATE = HD ** (-0.5) * math.log2(math.e)
F32 = jnp.float32
BF16 = jnp.bfloat16


def greet(peers):
    barrier = pltpu.get_barrier_semaphore()
    for peer in peers:
        pl.semaphore_signal(barrier, inc=1, device_id=peer, device_id_type=MESH)
    pl.semaphore_wait(barrier, len(peers))


def split_parts(width):
    half = width // 2
    return (
        (0, half, True, F32),
        (half, half, False, F32),
        (width, width, True, BF16),
        (2 * width, width, False, BF16),
    )


def project_kernel(ns, nh, nk, tok, w, q_out, kv_out, *scratch):
    (tokg, wboth, xs, xr, qall, zs, zr, ws, wr, wl, as_, ar, al, qs, qr) = scratch[:15]
    rest = scratch[15:]
    s, h, k = lax.axis_index("section"), lax.axis_index("head"), lax.axis_index("kv")
    nx = ns // 2
    x, c = s // 2, lax.rem(s, 2)
    rows, width = tok.shape
    depth = w.shape[0]

    def at_x(dx):
        return lax.rem(x + dx, nx)

    def at_k(dk):
        return lax.rem(k + dk, nk)

    offsets = [(dx, dk) for dx in range(nx) for dk in range(nk)]
    z_peers = [{"head": lax.rem(h + d, nh)} for d in range(1, nh)]
    core_peer = {"section": 2 * x + 1 - c}
    plane = {o: {"section": 2 * at_x(o[0]) + c, "kv": at_k(o[1])} for o in offsets}
    greet(z_peers + [core_peer] + [plane[o] for o in offsets if o != (0, 0)])

    pending = []

    def send(src, dst, ss, rs, peer):
        copy = pltpu.make_async_remote_copy(
            src_ref=src, dst_ref=dst, send_sem=ss, recv_sem=rs, device_id=peer, device_id_type=MESH
        )
        copy.start()
        pending.append(copy)
        return copy

    z_copies = [
        send(tok, tokg.at[d], zs.at[d], zr.at[d], z_peers[d]) for d in range(nh - 1)
    ]
    w_copy = send(w, wboth.at[c], ws, wr, core_peer)
    w_local = pltpu.make_async_copy(w, wboth.at[c], wl)
    w_local.start()

    own = tok[...].astype(F32)
    squares = jnp.sum(own * own, axis=1, keepdims=True)
    for d in range(nh - 1):
        z_copies[d].wait_recv()
        part = tokg[d].astype(F32)
        squares = squares + jnp.sum(part * part, axis=1, keepdims=True)
    factor = lax.rsqrt(squares * (1.0 / (width * nh)) + 1e-05)
    per_slot = width // depth

    def place(index, values):
        section, kv = index // nk, lax.rem(index, nk)
        xs[(section // 2) * nk + kv, :, pl.ds(pl.multiple_of(lax.rem(section, 2) * depth, depth), depth)] = values

    for d in range(nh):
        block = tok[...] if d == 0 else tokg[d - 1]
        scaled = (block.astype(F32) * factor).astype(BF16)
        origin = lax.rem(h + nh - d, nh)
        for j in range(per_slot):
            place(origin * per_slot + j, scaled[:, j * depth:(j + 1) * depth])

    a_copies = []
    mine = x * nk + k
    for i, o in enumerate(offsets):
        if o == (0, 0):
            continue
        a_copies.append(
            send(xs.at[at_x(o[0]) * nk + at_k(o[1])], xr.at[mine], as_.at[i], ar.at[i], plane[o])
        )
    a_local = pltpu.make_async_copy(xs.at[mine], xr.at[mine], al)
    a_local.start()
    w_local.wait()
    w_copy.wait_recv()
    a_local.wait()
    for copy in a_copies:
        copy.wait_recv()

    parts = split_parts(width)
    hop1 = []
    per = len(rest) // len(parts)
    bufs = [rest[i * per:(i + 1) * per] for i in range(len(parts))]
    inputs = xr[...].reshape(nx * nk * rows, 2 * depth)
    for (start, cols, x_first, kind), (full, out1, in1, out2, in2, sems) in zip(parts, bufs):
        step = min(cols, 512)
        for t in range(0, cols, step):
            piece = pl.ds(start + t, step)
            total = jnp.dot(inputs[:, :depth], wboth[0, :, piece], preferred_element_type=F32)
            total = total + jnp.dot(inputs[:, depth:], wboth[1, :, piece], preferred_element_type=F32)
            full[:, :, :, t:t + step] = total.reshape(nx, nk, rows, step)
        n1, n2 = (nx, nk) if x_first else (nk, nx)
        copies = []
        for d in range(1, n1):
            if x_first:
                out1[d - 1] = full[at_x(d)].astype(kind)
                peer = plane[(d, 0)]
            else:
                for xx in range(nx):
                    out1[d - 1, xx] = full[xx, at_k(d)].astype(kind)
                peer = plane[(0, d)]
            copies.append(send(out1.at[d - 1], in1.at[d - 1], sems.at[0, d], sems.at[1, d], peer))
        hop1.append(copies)

    hop2 = []
    for (start, cols, x_first, kind), (full, out1, in1, out2, in2, sems), copies in zip(parts, bufs, hop1):
        n1, n2 = (nx, nk) if x_first else (nk, nx)
        for copy in copies:
            copy.wait_recv()
        second = []

        def summed(other):
            total = full[x, other] if x_first else full[other, k]
            for d in range(n1 - 1):
                total = total + in1[d, other].astype(F32)
            return total

        for d in range(1, n2):
            other = at_k(d) if x_first else at_x(d)
            peer = plane[(0, d)] if x_first else plane[(d, 0)]
            out2[d - 1] = summed(other).astype(kind)
            second.append(send(out2.at[d - 1], in2.at[d - 1], sems.at[2, d], sems.at[3, d], peer))
        hop2.append((summed(k if x_first else x), second))

    q_copies = []
    for i, ((start, cols, x_first, kind), (full, out1, in1, out2, in2, sems)) in enumerate(zip(parts, bufs)):
        total, second = hop2[i]
        for d, copy in enumerate(second):
            copy.wait_recv()
            total = total + in2[d].astype(F32)
        if start < width:
            qall[k, :, start:start + cols] = total.astype(BF16)
            if start + cols == width:
                for d in range(1, nk):
                    q_copies.append(
                        send(qall.at[k], qall.at[k], qs.at[d], qr.at[d], plane[(0, d)])
                    )
        else:
            kv_out[:, start - width:start - width + cols] = total.astype(BF16)
    for copy in q_copies:
        copy.wait_recv()
    for copy in pending:
        copy.wait_send()
    q_out[...] = qall[...].reshape(nk * rows, width)


def project(ns, nh, nk, tokens, weights):
    rows, width = tokens.shape
    depth = weights.shape[0]
    nx = ns // 2
    dma = pltpu.SemaphoreType.DMA
    scratch = [
        pltpu.VMEM((nh - 1, rows, width), BF16),
        pltpu.VMEM((2, depth, 3 * width), BF16),
        pltpu.VMEM((nx * nk, rows, 2 * depth), BF16),
        pltpu.VMEM((nx * nk, rows, 2 * depth), BF16),
        pltpu.VMEM((nk, rows, width), BF16),
        dma((nh - 1,)), dma((nh - 1,)), dma, dma, dma,
        dma((nx * nk,)), dma((nx * nk,)), dma,
        dma((nk,)), dma((nk,)),
    ]
    for start, cols, x_first, kind in split_parts(width):
        n1, n2 = (nx, nk) if x_first else (nk, nx)
        scratch += [
            pltpu.VMEM((nx, nk, rows, cols), F32),
            pltpu.VMEM((max(n1 - 1, 1), n2, rows, cols), kind),
            pltpu.VMEM((max(n1 - 1, 1), n2, rows, cols), kind),
            pltpu.VMEM((max(n2 - 1, 1), rows, cols), kind),
            pltpu.VMEM((max(n2 - 1, 1), rows, cols), kind),
            dma((4, max(n1, n2))),
        ]
    vmem = pl.BlockSpec(memory_space=pltpu.VMEM)
    return pl.pallas_call(
        functools.partial(project_kernel, ns, nh, nk),
        out_shape=(
            jax.ShapeDtypeStruct((nk * rows, width), BF16),
            jax.ShapeDtypeStruct((rows, 2 * width), BF16),
        ),
        in_specs=[vmem, vmem],
        out_specs=(vmem, vmem),
        scratch_shapes=scratch,
        compiler_params=pltpu.CompilerParams(
            collective_id=0, has_side_effects=True, vmem_limit_bytes=56 * 1024 * 1024
        ),
        name="project",
    )(tokens, weights)


def attend_kernel(q_ref, ck_ref, cv_ref, nk_ref, nv_ref, start_ref, end_ref, mix_ref, peak_ref, total_ref):
    part, head = pl.program_id(0), pl.program_id(1)
    kv = lax.axis_index("kv")
    block, keys, news = q_ref.shape[0], ck_ref.shape[0], nk_ref.shape[0]
    contract = (((1,), (1,)), ((), ()))
    queries = q_ref[...]
    place = kv * keys + lax.broadcasted_iota(jnp.int32, (1, keys), 1)
    bias = jnp.where((place >= start_ref[0]) & (place < end_ref[0]), 0.0, LOW)
    old = lax.dot_general(queries, ck_ref[...], contract, preferred_element_type=F32) + bias
    new = lax.dot_general(queries, nk_ref[...], contract, preferred_element_type=F32)
    new_place = kv * news + lax.broadcasted_iota(jnp.int32, (block, news), 1)
    query_place = part * block + lax.broadcasted_iota(jnp.int32, (block, news), 0)
    new = jnp.where(new_place <= query_place, new, LOW)
    peak = jnp.maximum(
        jnp.max(old, axis=1, keepdims=True), jnp.max(new, axis=1, keepdims=True)
    )
    peak = jnp.maximum(peak, FLOOR)
    old_weights = jnp.exp2((old - peak) * RATE).astype(BF16)
    new_weights = jnp.exp2((new - peak) * RATE).astype(BF16)
    total = jnp.sum(old_weights.astype(F32), axis=1, keepdims=True) + jnp.sum(
        new_weights.astype(F32), axis=1, keepdims=True
    )
    mix_ref[...] = jnp.dot(old_weights, cv_ref[...], preferred_element_type=F32) + jnp.dot(
        new_weights, nv_ref[...], preferred_element_type=F32
    )
    lane = lax.broadcasted_iota(jnp.int32, peak_ref.shape, 1)

    @pl.when(head == 0)
    def _():
        peak_ref[...] = jnp.zeros_like(peak_ref)
        total_ref[...] = jnp.zeros_like(total_ref)

    peak_ref[...] = jnp.where(lane == head, peak, peak_ref[...])
    total_ref[...] = jnp.where(lane == head, total, total_ref[...])


def attend(queries, cache_keys, cache_values, new_pair, key_start, key_end):
    count, width = queries.shape
    heads = width // HD
    keys, news = cache_keys.shape[1], new_pair.shape[0]
    block = 256 if count % 256 == 0 else count
    smem = pl.BlockSpec(memory_space=pltpu.SMEM)
    return pl.pallas_call(
        attend_kernel,
        grid=(count // block, heads),
        out_shape=(
            jax.ShapeDtypeStruct((count, width), F32),
            jax.ShapeDtypeStruct((count, HD), F32),
            jax.ShapeDtypeStruct((count, HD), F32),
        ),
        in_specs=[
            pl.BlockSpec((block, HD), lambda i, n: (i, n)),
            pl.BlockSpec((None, keys, HD), lambda i, n: (0, 0, n)),
            pl.BlockSpec((None, keys, HD), lambda i, n: (0, 0, n)),
            pl.BlockSpec((news, HD), lambda i, n: (0, n)),
            pl.BlockSpec((news, HD), lambda i, n: (0, heads + n)),
            smem,
            smem,
        ],
        out_specs=(
            pl.BlockSpec((block, HD), lambda i, n: (i, n)),
            pl.BlockSpec((block, HD), lambda i, n: (i, 0)),
            pl.BlockSpec((block, HD), lambda i, n: (i, 0)),
        ),
        compiler_params=pltpu.CompilerParams(vmem_limit_bytes=48 * 1024 * 1024),
        name="attend",
    )(queries, cache_keys, cache_values, new_pair, new_pair, key_start, key_end)


def finish_kernel(nh, nk, mix, peaks, totals, w_hbm, out, w, mixs, mixr, pr, tr, terms, got, wl, ms, mr, ps, prs, ts, trs, os, ors):
    h, k = lax.axis_index("head"), lax.axis_index("kv")
    rows, width = out.shape
    heads = width // HD
    kv_peers = [{"kv": lax.rem(k + d, nk)} for d in range(1, nk)]
    z_peers = [{"head": lax.rem(h + d, nh)} for d in range(1, nh)]
    load = pltpu.make_async_copy(w_hbm, w, wl)
    load.start()
    greet(kv_peers + z_peers)
    pending = []

    def send(src, dst, ss, rs, peer):
        copy = pltpu.make_async_remote_copy(
            src_ref=src, dst_ref=dst, send_sem=ss, recv_sem=rs, device_id=peer, device_id_type=MESH
        )
        copy.start()
        pending.append(copy)
        return copy

    arrivals = []
    for d in range(1, nk):
        theirs = pl.ds(pl.multiple_of(lax.rem(k + d, nk) * rows, rows), rows)
        mixs[d - 1] = mix[theirs].astype(BF16)
        peer = kv_peers[d - 1]
        arrivals.append(send(peaks.at[theirs], pr.at[d - 1], ps.at[d], prs.at[d], peer))
        arrivals.append(send(totals.at[theirs], tr.at[d - 1], ts.at[d], trs.at[d], peer))
        arrivals.append(send(mixs.at[d - 1], mixr.at[d - 1], ms.at[d], mr.at[d], peer))
    for copy in arrivals:
        copy.wait_recv()
    mine = pl.ds(pl.multiple_of(k * rows, rows), rows)
    own_peak, own_total = peaks[mine], totals[mine]
    highest = own_peak
    for d in range(nk - 1):
        highest = jnp.maximum(highest, pr[d])
    factors = [jnp.exp2((own_peak - highest) * RATE)]
    total = own_total * factors[0]
    for d in range(nk - 1):
        factors.append(jnp.exp2((pr[d] - highest) * RATE))
        total = total + tr[d] * factors[-1]
    columns = []
    for n in range(heads):
        cols = pl.ds(n * HD, HD)
        value = mix[mine, cols] * factors[0][:, n:n + 1]
        for d in range(nk - 1):
            value = value + mixr[d, :, cols].astype(F32) * factors[d + 1][:, n:n + 1]
        columns.append((value / total[:, n:n + 1]).astype(BF16))
    attended = jnp.concatenate(columns, axis=1)
    load.wait()
    copies = []
    for d in range(1, nh):
        target = lax.rem(h + d, nh)
        cols = pl.ds(pl.multiple_of(target * width, width), width)
        terms[d - 1] = jnp.dot(attended, w[:, cols], preferred_element_type=F32).astype(BF16)
        copies.append(send(terms.at[d - 1], got.at[d - 1], os.at[d], ors.at[d], z_peers[d - 1]))
    cols = pl.ds(pl.multiple_of(h * width, width), width)
    result = jnp.dot(attended, w[:, cols], preferred_element_type=F32)
    for d, copy in enumerate(copies):
        copy.wait_recv()
        result = result + got[d].astype(F32)
    out[...] = result.astype(BF16)
    for copy in pending:
        copy.wait_send()


def finish(nh, nk, mix, peaks, totals, w_out):
    count, width = mix.shape
    rows = count // nk
    dma = pltpu.SemaphoreType.DMA
    vmem = pl.BlockSpec(memory_space=pltpu.VMEM)
    more = max(nk - 1, 1)
    return pl.pallas_call(
        functools.partial(finish_kernel, nh, nk),
        out_shape=jax.ShapeDtypeStruct((rows, width), BF16),
        in_specs=[vmem, vmem, vmem, pl.BlockSpec(memory_space=pl.ANY)],
        out_specs=vmem,
        scratch_shapes=[
            pltpu.VMEM(w_out.shape, BF16),
            pltpu.VMEM((more, rows, width), BF16),
            pltpu.VMEM((more, rows, width), BF16),
            pltpu.VMEM((more, rows, HD), F32),
            pltpu.VMEM((more, rows, HD), F32),
            pltpu.VMEM((max(nh - 1, 1), rows, width), BF16),
            pltpu.VMEM((max(nh - 1, 1), rows, width), BF16),
            dma,
            dma((nk,)), dma((nk,)), dma((nk,)), dma((nk,)), dma((nk,)), dma((nk,)),
            dma((nh,)), dma((nh,)),
        ],
        compiler_params=pltpu.CompilerParams(
            collective_id=1, has_side_effects=True, vmem_limit_bytes=48 * 1024 * 1024
        ),
        name="finish",
    )(mix, peaks, totals, w_out)


def shards(ns, nh, nk, tokens, w_query, w_keyvalue, cache_keys, cache_values, key_start, key_end, w_out):
    weights = jnp.concatenate([w_query, w_keyvalue[:, 0, :], w_keyvalue[:, 1, :]], axis=1)
    w_full = lax.all_gather(w_out, ("section", "kv"), axis=1, tiled=True)
    queries, new_pair = project(ns, nh, nk, tokens[0], weights)
    mix, peaks, totals = attend(queries, cache_keys, cache_values, new_pair, key_start, key_end)
    return finish(nh, nk, mix, peaks, totals, w_full)[None]


def solution(mesh):
    placed = (
        P("section", "kv", "head"),
        P(("section", "kv"), "head"),
        P(("section", "kv"), None, "head"),
        P("section", "kv", "head"),
        P("section", "kv", "head"),
        P("section"),
        P("section"),
        P("head", ("section", "kv")),
    )
    body = functools.partial(shards, mesh.shape["section"], mesh.shape["head"], mesh.shape["kv"])
    return jax.shard_map(
        body, mesh=mesh, in_specs=placed, out_specs=P("section", "kv", "head"), check_vma=False
    )
```

time: 328 us -> 172 us (0.52)
  waiting for transfers between devices: 201 us -> 0.73 us
  Pallas kernels: 0 us -> 143 us
  matrix products: 32 us -> 0 us
  local copies, waits for them, and re-layouts: 37.7 us -> 9.57 us
  other arithmetic: 16.8 us -> 1.83 us
  starting transfers between devices: 11.7 us -> 0.01 us
  blocking collectives: 10.2 us -> 0 us
    all_gather x4 -> x1, waiting for transfers between devices: 144 us -> 0.02 us  [shards(): w_full = lax.all_gather(w_out, ('section', 'kv'), axis=1, tiled=True)]
    pallas_call x0 -> x3, Pallas kernels: none -> 143 us  [the longest x1 96.7 us: project(): pl.pallas_call(functools.partial(project_kernel, ns, nh, nk), out_shape=(...]
    reduce_scatter x1 -> x0, waiting for transfers between devices: 43.5 us -> none  [shards(): summed = lax.psum_scatter(terms, 'head', scatter_dimension=1, tiled=True)]
    dot_general x5 -> x0, matrix products: 32 us -> none  [the longest x1 10.3 us: attend(): jnp.einsum('hqk,khd->qhd', weights, values_all, preferred_element_type=jn...]
    unnamed x13 -> x7, local copies, waits for them, and re-layouts: 27.6 us -> 3.17 us
    reduce_sum x4 -> x0, other arithmetic: 11.7 us -> none  [the longest x1 8.75 us: attend(): row_total = jnp.sum(weights.astype(jnp.float32), axis=2)]
    all_to_all x3 -> x0, starting transfers between devices: 11.5 us -> none  [the longest x1 4.57 us: shards(): lax.all_to_all(totals[None], 'kv', split_axis=1, concat_axis=0, tiled=True)]
    all_to_all x3 -> x0, waiting for transfers between devices: 10.6 us -> none  [the longest x1 10.6 us: shards(): lax.all_to_all(mixtures[None], 'kv', split_axis=1, concat_axis=0, tiled=T...]
  transfers between devices with their start and end apart: 8 -> 1, of which waited for: 5 -> 0; matrix products, arithmetic and copies ran while one was open for 24% -> 5% of each run, Pallas kernels for 0% -> 64%
where the time goes in v1:
time: 172 us; the launch traced here: 170 us
  Pallas kernels  143 us (83%)
  between operations  14.7 us (9%)
  local copies, waits for them, and re-layouts  9.57 us (6%)
  other arithmetic  1.83 us (1%)
    pallas_call x1, Pallas kernels, project(): pl.pallas_call(functools.partial(project_kernel, ns, nh, nk), out_shape=(...  96.7 us
    pallas_call x1, Pallas kernels, finish(): pl.pallas_call(functools.partial(finish_kernel, nh, nk), out_shape=jax.Sh...  34.1 us
    pallas_call x1, Pallas kernels, attend(): pl.pallas_call(attend_kernel, grid=(count // block, heads), out_shape=(ja...  12.4 us
    slice x1, local copies, waits for them, and re-layouts, shards(): w_keyvalue[:, 0, :]  5.58 us
  transfers between devices with their start and end apart: 1, of which 0 were waited for; matrix products, arithmetic and copies ran while one was open for 5% of the time, Pallas kernels for 64%

profile of v1, /device:TPU:28, one launch (start us, length us, event | category | flops | bytes accessed | tf_op | source)
XLA Modules:
  0.0 170.0 jit_solution(7481201535469569788)
XLA Ops:
  6.5 0.0 all-gather.2.cloned.1.call-start
  6.5 0.7 all-gather.2.cloned.1.call-update
  8.5 5.6 %fusion = (bf16[512,1,1024]{2,1,0:T(2,128)(2,1)S(1)}, bf16[512,1,1024]{2,1,0:T(2,128)(2,1)S(1)}) fusion(bf16[512,2,1024]{2,1,0:T(2,128)(2,1)} %param.10), kind=kLoop, calls=%fused_computation.3 | loop fusion | bytes 4194304 | tf_op jit(solution)/shard_map/slice | solution.py:384
  14.1 0.0 copy-start.2
  14.1 0.8 copy_bitcast_fusion
  15.0 0.4 copy-done.2
  15.4 1.8 %pad_maximum_fusion.w = bf16[512,3072]{1,0:T(8,128)(2,1)} fusion(bf16[512,1024]{1,0:T(8,128)(2,1)S(1)} %get-tuple-element.17, bf16[512,1024]{1,0:T(8,128)(2,1)S(1)} %get-tuple-element.18, bf16[512,1024]{1,0:T(8,128)(2,1)S(1)} %copy-done.2), kind=kLoop, calls=%fused_computation | loop fusion | flops 9437184 | bytes 6291456 | tf_op jit(solution)/shard_map/concatenate | solution.py:384
  17.2 96.7 %project.1 = (bf16[256,1024]{1,0:T(8,128)(2,1)}, bf16[128,2048]{1,0:T(8,128)(2,1)}) custom-call(bf16[128,1024]{1,0:T(8,128)(2,1)} %bitcast.7, bf16[512,3072]{1,0:T(8,128)(2,1)} %pad_maximum_fusion.w), custom_call_target="tpu_custom_call" | custom-call | tf_op jit(solution)/shard_map/project/pallas_call | solution.py:204
  113.9 0.0 copy-start
  113.9 1.0 copy-done
  114.9 0.0 copy-start.1
  114.9 1.0 copy-done.1
  115.9 12.4 %attend.1 = (f32[256,1024]{1,0:T(8,128)S(1)}, f32[256,128]{1,0:T(8,128)S(1)}, f32[256,128]{1,0:T(8,128)S(1)}) custom-call(bf16[256,1024]{1,0:T(8,128)(2,1)S(1)} %copy-done.1, bf16[1,2048,1024]{2,1,0:T(8,128)(2,1)} %ck_ref.1, bf16[1,2048,1024]{2,1,0:T(8,128)(2,1)} %cv_ref.1, bf16[128,2048]{1,0:T(8,128)(2,1)S(1)} %copy-done, bf16[128,2048]{1,0:T(8,128)(2,1)S(1)} %copy-done, ...), custom_call_target="tpu_custom_call" | custom-call | tf_op jit(solution)/shard_map/attend/pallas_call | solution.py:262
  128.3 0.0 all-gather.2.cloned.1.call-done.w_hbm
  128.4 34.1 %finish.1 = bf16[128,1024]{1,0:T(8,128)(2,1)S(1)} custom-call(f32[256,1024]{1,0:T(8,128)S(1)} %get-tuple-element.12.mix, f32[256,128]{1,0:T(8,128)S(1)} %get-tuple-element.13.peaks, f32[256,128]{1,0:T(8,128)S(1)} %get-tuple-element.14.totals, bf16[1024,4096]{1,0:T(8,128)(2,1)} %all-gather.2.cloned.1.call-done.w_hbm), custom_call_target="tpu_custom_call" | custom-call | tf_op jit(solution)/shard_map/finish/pallas_call | solution.py:359
  162.5 0.7 copy.18
Async XLA Ops:
  6.5 121.8 %all-gather.2.cloned.1.call-start = ((), (), s32[]{:S(2)}) async-start(), calls=%async_computation | async-start | bytes 9437184 | tf_op jit(solution)/shard_map/all_gather | solution.py:385
  14.1 1.2 copy-start.2
  113.9 1.0 copy-start
  114.9 1.0 copy-start.1
Sparse Core Ops, SparseCore 0:
  9.2 68.6 all-gather.1

commit v2 on v1

v2 whole, which is shorter than its diff:
```python
import functools
import math

import jax
import jax.numpy as jnp
from jax import lax
from jax.experimental import pallas as pl
from jax.experimental.pallas import tpu as pltpu
from jax.sharding import PartitionSpec as P

HD = 128
MESH = pl.DeviceIdType.MESH
LOW = -1e30
FLOOR = -1e29
RATE = HD ** (-0.5) * math.log2(math.e)
F32 = jnp.float32
BF16 = jnp.bfloat16


def greet(peers):
    barrier = pltpu.get_barrier_semaphore()
    for peer in peers:
        pl.semaphore_signal(barrier, inc=1, device_id=peer, device_id_type=MESH)
    pl.semaphore_wait(barrier, len(peers))


def split_parts(width):
    half = width // 2
    return (
        (0, half, True, F32),
        (half, half, False, F32),
        (width, width, True, BF16),
        (2 * width, width, False, BF16),
    )


def block_kernel(
    ns, nh, nk, tok, wq, wk, wv, ck_hbm, cv_hbm, start_ref, end_ref, out,
    tokg, wboth, xr, xn, facs, facr, qall, ck, cv, pair, mix, stat, mixs, mixr, statr,
    zs, zr, ws, wr, wl, fs, fr, gs, gr, qs, qr, cl, ms, mr, ss_, sr_, *rest
):
    s, h, k = lax.axis_index("section"), lax.axis_index("head"), lax.axis_index("kv")
    nx = ns // 2
    x, c = s // 2, lax.rem(s, 2)
    rows, width = tok.shape
    depth = wq.shape[0]
    heads = width // HD
    keys = ck.shape[0]
    mine = x * nk + k
    per_slot = width // depth

    def at_x(dx):
        return lax.rem(x + dx, nx)

    def at_k(dk):
        return lax.rem(k + dk, nk)

    offsets = [(dx, dk) for dx in range(nx) for dk in range(nk)]
    z_peers = [{"head": lax.rem(h + d, nh)} for d in range(1, nh)]
    core_peer = {"section": 2 * x + 1 - c}
    plane = {o: {"section": 2 * at_x(o[0]) + c, "kv": at_k(o[1])} for o in offsets}
    greet(z_peers + [core_peer] + [plane[o] for o in offsets if o != (0, 0)])

    pending = []

    def send(src, dst, send_sem, recv_sem, peer):
        copy = pltpu.make_async_remote_copy(
            src_ref=src, dst_ref=dst, send_sem=send_sem, recv_sem=recv_sem, device_id=peer, device_id_type=MESH
        )
        copy.start()
        pending.append(copy)
        return copy

    z_copies = [
        send(tok, tokg.at[d], zs.at[d], zr.at[d], z_peers[d]) for d in range(nh - 1)
    ]

    forwards = []

    def forward(d, block):
        origin = lax.rem(h + nh - d, nh)
        for j in range(per_slot):
            index = origin * per_slot + j
            section, kv = index // nk, lax.rem(index, nk)
            core = lax.rem(section, 2)
            src = block.at[:, pl.ds(j * depth, depth)]
            dst = xr.at[mine, core]
            here = (section // 2 == x) & (kv == k)
            far = pltpu.make_async_remote_copy(
                src_ref=src, dst_ref=dst, send_sem=gs.at[d, j], recv_sem=gr.at[mine, core],
                device_id={"section": (section // 2) * 2 + c, "kv": kv}, device_id_type=MESH,
            )
            near = pltpu.make_async_copy(src, dst, gr.at[mine, core])

            @pl.when(here)
            def _():
                near.start()

            @pl.when(jnp.logical_not(here))
            def _():
                far.start()

            forwards.append((here, far))

    forward(0, tok)
    w_copies, w_locals = [], []
    for i, w in enumerate((wq, wk, wv)):
        spot = wboth.at[c, :, pl.ds(i * width, width)]
        w_copies.append(send(w, spot, ws.at[i], wr.at[i], core_peer))
        local = pltpu.make_async_copy(w, spot, wl.at[i])
        local.start()
        w_locals.append(local)
    loads = [
        pltpu.make_async_copy(ck_hbm.at[0], ck, cl.at[0]),
        pltpu.make_async_copy(cv_hbm.at[0], cv, cl.at[1]),
    ]
    for load in loads:
        load.start()

    own = tok[...].astype(F32)
    squares = jnp.sum(own * own, axis=1, keepdims=True)
    for d in range(1, nh):
        z_copies[d - 1].wait_recv()
        forward(d, tokg.at[d - 1])
        part = tokg[d - 1].astype(F32)
        squares = squares + jnp.sum(part * part, axis=1, keepdims=True)
    factor = lax.rsqrt(squares * (1.0 / (width * nh)) + 1e-05)
    facs[...] = jnp.broadcast_to(factor, (rows, HD))
    facr[mine] = facs[...]
    f_copies = []
    for i, o in enumerate(offsets):
        if o != (0, 0):
            f_copies.append(send(facs, facr.at[mine], fs.at[i], fr.at[i], plane[o]))
    for copy in w_copies:
        copy.wait_recv()
    for copy in w_locals:
        copy.wait()
    for g in range(nx * nk):
        for core in range(2):
            pltpu.make_async_copy(xr.at[g, core], xr.at[g, core], gr.at[g, core]).wait()
    for copy in f_copies:
        copy.wait_recv()
    for g in range(nx * nk):
        scale = facr[g][:, :1]
        for core in range(2):
            xn[core, pl.ds(g * rows, rows), :] = (xr[g, core].astype(F32) * scale).astype(BF16)

    parts = split_parts(width)
    per = len(rest) // len(parts)
    bufs = [rest[i * per:(i + 1) * per] for i in range(len(parts))]

    def multiply(i):
        start, cols, x_first, kind = parts[i]
        full, out1 = bufs[i][:2]
        step = min(cols, 512)
        for t in range(0, cols, step):
            piece = pl.ds(start + t, step)
            total = jnp.dot(xn[0], wboth[0, :, piece], preferred_element_type=F32)
            total = total + jnp.dot(xn[1], wboth[1, :, piece], preferred_element_type=F32)
            full[:, :, :, t:t + step] = total.reshape(nx, nk, rows, step)
        for d in range(1, nx if x_first else nk):
            if x_first:
                out1[d - 1] = full[at_x(d)].astype(kind)
            else:
                for xx in range(nx):
                    out1[d - 1, xx] = full[xx, at_k(d)].astype(kind)

    def first_hop(i):
        x_first = parts[i][2]
        full, out1, in1, out2, in2, sems = bufs[i]
        return [
            send(out1.at[d - 1], in1.at[d - 1], sems.at[0, d], sems.at[1, d], plane[(d, 0) if x_first else (0, d)])
            for d in range(1, nx if x_first else nk)
        ]

    def second_hop(i, copies):
        start, cols, x_first, kind = parts[i]
        full, out1, in1, out2, in2, sems = bufs[i]
        n1, n2 = (nx, nk) if x_first else (nk, nx)
        for copy in copies:
            copy.wait_recv()

        def summed(other):
            total = full[x, other] if x_first else full[other, k]
            for d in range(n1 - 1):
                total = total + in1[d, other].astype(F32)
            return total

        second = []
        for d in range(1, n2):
            out2[d - 1] = summed(at_k(d) if x_first else at_x(d)).astype(kind)
            peer = plane[(0, d) if x_first else (d, 0)]
            second.append(send(out2.at[d - 1], in2.at[d - 1], sems.at[2, d], sems.at[3, d], peer))
        return summed(k if x_first else x), second

    def last(i, total, second):
        in2 = bufs[i][4]
        for d, copy in enumerate(second):
            copy.wait_recv()
            total = total + in2[d].astype(F32)
        return total.astype(BF16)

    half = width // 2
    multiply(0)
    hop_a = first_hop(0)
    multiply(1)
    hop_b = first_hop(1)
    multiply(2)
    multiply(3)
    sum_a = second_hop(0, hop_a)
    sum_b = second_hop(1, hop_b)
    qall[k, :, :half] = last(0, *sum_a)
    qall[k, :, half:] = last(1, *sum_b)
    q_copies = [
        send(qall.at[k], qall.at[k], qs.at[d], qr.at[d], plane[(0, d)]) for d in range(1, nk)
    ]
    hop_k = first_hop(2)
    hop_v = first_hop(3)
    for load in loads:
        load.wait()

    contract = (((1,), (1,)), ((), ()))
    place = k * keys + lax.broadcasted_iota(jnp.int32, (1, keys), 1)
    bias = jnp.where((place >= start_ref[0]) & (place < end_ref[0]), 0.0, LOW)
    lane = lax.broadcasted_iota(jnp.int32, (rows, HD), 1)

    def resident(block, begin, end):
        @pl.loop(begin, end)
        def _(n):
            cols = pl.ds(pl.multiple_of(n * HD, HD), HD)
            scores = lax.dot_general(
                qall[block, :, cols], ck[:, cols], contract, preferred_element_type=F32
            ) + bias
            peak = jnp.maximum(jnp.max(scores, axis=1, keepdims=True), FLOOR)
            weights = jnp.exp2((scores - peak) * RATE).astype(BF16)
            total = jnp.sum(weights.astype(F32), axis=1, keepdims=True)
            mix[block, :, cols] = jnp.dot(weights, cv[:, cols], preferred_element_type=F32)
            stat[block] = jnp.where(lane == n, peak, jnp.where(lane == n + HD // 2, total, stat[block]))

    def fresh(block, target):
        query_place = block * rows + lax.broadcasted_iota(jnp.int32, (rows, rows), 0)
        new_place = k * rows + lax.broadcasted_iota(jnp.int32, (rows, rows), 1)
        usable = new_place <= query_place
        stats = stat[block]
        merged = stats
        for n in range(heads):
            cols = pl.ds(n * HD, HD)
            scores = lax.dot_general(
                qall[block, :, cols], pair[:, cols], contract, preferred_element_type=F32
            )
            scores = jnp.where(usable, scores, LOW)
            before = stats[:, n:n + 1]
            peak = jnp.maximum(before, jnp.max(scores, axis=1, keepdims=True))
            weights = jnp.exp2((scores - peak) * RATE).astype(BF16)
            shrink = jnp.exp2((before - peak) * RATE)
            total = stats[:, n + HD // 2:n + HD // 2 + 1] * shrink + jnp.sum(
                weights.astype(F32), axis=1, keepdims=True
            )
            value = mix[block, :, cols] * shrink + jnp.dot(
                weights, pair[:, pl.ds(width + n * HD, HD)], preferred_element_type=F32
            )
            if target is None:
                mix[block, :, cols] = value
            else:
                target[:, cols] = value.astype(BF16)
            merged = jnp.where(lane == n, peak, jnp.where(lane == n + HD // 2, total, merged))
        stat[block] = merged

    stat[...] = jnp.zeros_like(stat)
    resident(k, 0, heads)
    for copy in q_copies:
        copy.wait_recv()
    for d in range(1, nk - 1):
        resident(at_k(d), 0, heads)
    if nk > 1:
        resident(at_k(nk - 1), 0, heads // 2)
    sum_k = second_hop(2, hop_k)
    sum_v = second_hop(3, hop_v)
    if nk > 1:
        resident(at_k(nk - 1), heads // 2, heads)
    pair[:, :width] = last(2, *sum_k)
    pair[:, width:] = last(3, *sum_v)
    arrivals = []
    for d in range(1, nk):
        other = at_k(d)
        fresh(other, mixs.at[d - 1])
        arrivals.append(send(stat.at[other], statr.at[d - 1], ss_.at[d], sr_.at[d], plane[(0, d)]))
        arrivals.append(send(mixs.at[d - 1], mixr.at[d - 1], ms.at[d], mr.at[d], plane[(0, d)]))
    fresh(k, None)
    for copy in arrivals:
        copy.wait_recv()

    def tops(stats):
        return stats[:, :heads]

    def sums(stats):
        return stats[:, HD // 2:HD // 2 + heads]

    own_stat = stat[k]
    highest = tops(own_stat)
    for d in range(nk - 1):
        highest = jnp.maximum(highest, tops(statr[d]))
    factors = [jnp.exp2((tops(own_stat) - highest) * RATE)]
    total = sums(own_stat) * factors[0]
    for d in range(nk - 1):
        factors.append(jnp.exp2((tops(statr[d]) - highest) * RATE))
        total = total + sums(statr[d]) * factors[-1]
    for n in range(heads):
        cols = pl.ds(n * HD, HD)
        value = mix[k, :, cols] * factors[0][:, n:n + 1]
        for d in range(nk - 1):
            value = value + mixr[d, :, cols].astype(F32) * factors[d + 1][:, n:n + 1]
        out[:, cols] = (value / total[:, n:n + 1]).astype(BF16)

    for copy in pending:
        copy.wait_send()
    for here, far in forwards:
        @pl.when(jnp.logical_not(here))
        def _():
            far.wait_send()


def attend_block(ns, nh, nk, tokens, wq, wk, wv, cache_keys, cache_values, key_start, key_end):
    rows, width = tokens.shape
    depth = wq.shape[0]
    keys = cache_keys.shape[1]
    nx = ns // 2
    group = nx * nk
    more = max(nk - 1, 1)
    dma = pltpu.SemaphoreType.DMA
    scratch = [
        pltpu.VMEM((nh - 1, rows, width), BF16),
        pltpu.VMEM((2, depth, 3 * width), BF16),
        pltpu.VMEM((group, 2, rows, depth), BF16),
        pltpu.VMEM((2, group * rows, depth), BF16),
        pltpu.VMEM((rows, HD), F32),
        pltpu.VMEM((group, rows, HD), F32),
        pltpu.VMEM((nk, rows, width), BF16),
        pltpu.VMEM((keys, width), BF16),
        pltpu.VMEM((keys, width), BF16),
        pltpu.VMEM((rows, 2 * width), BF16),
        pltpu.VMEM((nk, rows, width), F32),
        pltpu.VMEM((nk, rows, HD), F32),
        pltpu.VMEM((more, rows, width), BF16),
        pltpu.VMEM((more, rows, width), BF16),
        pltpu.VMEM((more, rows, HD), F32),
        dma((nh - 1,)), dma((nh - 1,)),
        dma((3,)), dma((3,)), dma((3,)),
        dma((group,)), dma((group,)),
        dma((nh, width // depth)), dma((group, 2)),
        dma((nk,)), dma((nk,)),
        dma((2,)),
        dma((nk,)), dma((nk,)), dma((nk,)), dma((nk,)),
    ]
    for start, cols, x_first, kind in split_parts(width):
        n1, n2 = (nx, nk) if x_first else (nk, nx)
        scratch += [
            pltpu.VMEM((nx, nk, rows, cols), F32),
            pltpu.VMEM((max(n1 - 1, 1), n2, rows, cols), kind),
            pltpu.VMEM((max(n1 - 1, 1), n2, rows, cols), kind),
            pltpu.VMEM((max(n2 - 1, 1), rows, cols), kind),
            pltpu.VMEM((max(n2 - 1, 1), rows, cols), kind),
            dma((4, max(n1, n2))),
        ]
    vmem = pl.BlockSpec(memory_space=pltpu.VMEM)
    smem = pl.BlockSpec(memory_space=pltpu.SMEM)
    hbm = pl.BlockSpec(memory_space=pl.ANY)
    return pl.pallas_call(
        functools.partial(block_kernel, ns, nh, nk),
        out_shape=jax.ShapeDtypeStruct((rows, width), BF16),
        in_specs=[vmem, hbm, hbm, hbm, hbm, hbm, smem, smem],
        out_specs=vmem,
        scratch_shapes=scratch,
        compiler_params=pltpu.CompilerParams(
            collective_id=0, has_side_effects=True, vmem_limit_bytes=60 * 1024 * 1024
        ),
        name="attend_block",
    )(tokens, wq, wk, wv, cache_keys, cache_values, key_start, key_end)


def finish_kernel(nh, attended_ref, w_hbm, out, w, terms, got, wl, os, ors):
    h = lax.axis_index("head")
    rows, width = out.shape
    z_peers = [{"head": lax.rem(h + d, nh)} for d in range(1, nh)]
    load = pltpu.make_async_copy(w_hbm, w, wl)
    load.start()
    greet(z_peers)
    attended = attended_ref[...]
    load.wait()
    copies = []
    for d in range(1, nh):
        target = lax.rem(h + d, nh)
        cols = pl.ds(pl.multiple_of(target * width, width), width)
        terms[d - 1] = jnp.dot(attended, w[:, cols], preferred_element_type=F32).astype(BF16)
        copy = pltpu.make_async_remote_copy(
            src_ref=terms.at[d - 1], dst_ref=got.at[d - 1], send_sem=os.at[d], recv_sem=ors.at[d],
            device_id=z_peers[d - 1], device_id_type=MESH,
        )
        copy.start()
        copies.append(copy)
    cols = pl.ds(pl.multiple_of(h * width, width), width)
    result = jnp.dot(attended, w[:, cols], preferred_element_type=F32)
    for d, copy in enumerate(copies):
        copy.wait_recv()
        result = result + got[d].astype(F32)
    out[...] = result.astype(BF16)
    for copy in copies:
        copy.wait_send()


def finish(nh, attended, w_out):
    rows, width = attended.shape
    dma = pltpu.SemaphoreType.DMA
    vmem = pl.BlockSpec(memory_space=pltpu.VMEM)
    return pl.pallas_call(
        functools.partial(finish_kernel, nh),
        out_shape=jax.ShapeDtypeStruct((rows, width), BF16),
        in_specs=[vmem, pl.BlockSpec(memory_space=pl.ANY)],
        out_specs=vmem,
        scratch_shapes=[
            pltpu.VMEM(w_out.shape, BF16),
            pltpu.VMEM((max(nh - 1, 1), rows, width), BF16),
            pltpu.VMEM((max(nh - 1, 1), rows, width), BF16),
            dma, dma((nh,)), dma((nh,)),
        ],
        compiler_params=pltpu.CompilerParams(
            collective_id=1, has_side_effects=True, vmem_limit_bytes=48 * 1024 * 1024
        ),
        name="finish",
    )(attended, w_out)


def shards(ns, nh, nk, tokens, w_query, w_keyvalue, cache_keys, cache_values, key_start, key_end, w_out):
    w_full = lax.all_gather(w_out, ("section", "kv"), axis=1, tiled=True)
    attended = attend_block(
        ns, nh, nk, tokens[0], w_query, w_keyvalue[:, 0, :], w_keyvalue[:, 1, :],
        cache_keys, cache_values, key_start, key_end,
    )
    return finish(nh, attended, w_full)[None]


def solution(mesh):
    placed = (
        P("section", "kv", "head"),
        P(("section", "kv"), "head"),
        P(("section", "kv"), None, "head"),
        P("section", "kv", "head"),
        P("section", "kv", "head"),
        P("section"),
        P("section"),
        P("head", ("section", "kv")),
    )
    body = functools.partial(shards, mesh.shape["section"], mesh.shape["head"], mesh.shape["kv"])
    return jax.shard_map(
        body, mesh=mesh, in_specs=placed, out_specs=P("section", "kv", "head"), check_vma=False
    )
```

time: 172 us -> 163 us (0.948)
  Pallas kernels: 143 us -> 137 us
  other arithmetic: 1.83 us -> 0 us
    pallas_call x3 -> x2, Pallas kernels: 143 us -> 137 us  [the longest x1 116 us: attend_block(): pl.pallas_call(functools.partial(block_kernel, ns, nh, nk), out_shape=jax...]
    concatenate x1 -> x0, other arithmetic: 1.83 us -> none  [shards(): jnp.concatenate([w_query, w_keyvalue[:, 0, :], w_keyvalue[:, 1, :]], axis=1)]
  transfers between devices with their start and end apart: 1 -> 1, of which waited for: 0 -> 0; matrix products, arithmetic and copies ran while one was open for 5% -> 5% of each run, Pallas kernels for 64% -> 72%
where the time goes in v2:
time: 163 us; the launch traced here: 162 us
  Pallas kernels  137 us (84%)
  between operations  14.7 us (9%)
  local copies, waits for them, and re-layouts  9.33 us (6%)
    pallas_call x1, Pallas kernels, attend_block(): pl.pallas_call(functools.partial(block_kernel, ns, nh, nk), out_shape=jax...  116 us
    pallas_call x1, Pallas kernels, finish(): pl.pallas_call(functools.partial(finish_kernel, nh), out_shape=jax.ShapeD...  21.1 us
    slice x1, local copies, waits for them, and re-layouts, shards(): w_keyvalue[:, 1, :]  5.51 us
  transfers between devices with their start and end apart: 1, of which 0 were waited for; matrix products, arithmetic and copies ran while one was open for 5% of the time, Pallas kernels for 72%

profile of v2, /device:TPU:28, one launch (start us, length us, event | category | flops | bytes accessed | tf_op | source)
XLA Modules:
  0.0 161.7 jit_solution(846902480326317025)
XLA Ops:
  6.5 0.0 all-gather.2.cloned.1.call-start
  6.5 0.7 all-gather.2.cloned.1.call-update
  8.5 5.5 %fusion = (bf16[512,1,1024]{2,1,0:T(2,128)(2,1)S(1)}, bf16[512,1,1024]{2,1,0:T(2,128)(2,1)S(1)}) fusion(bf16[512,2,1024]{2,1,0:T(2,128)(2,1)} %param.10), kind=kLoop, calls=%fused_computation.2 | loop fusion | bytes 4194304 | tf_op jit(solution)/shard_map/slice | solution.py:436
  14.1 2.2 %copy_bitcast_fusion = (bf16[512,1024]{1,0:T(8,128)(2,1)}, bf16[512,1024]{1,0:T(8,128)(2,1)}) fusion(bf16[512,1,1024]{2,1,0:T(2,128)(2,1)S(1)} %get-tuple-element.5, bf16[512,1,1024]{2,1,0:T(2,128)(2,1)S(1)} %get-tuple-element.6), kind=kLoop, calls=%fused_computation | loop fusion | bytes 4194304 | tf_op jit(solution)/shard_map/squeeze | solution.py:436
  16.2 115.8 %attend_block.1.attended_ref = bf16[128,1024]{1,0:T(8,128)(2,1)} custom-call(bf16[128,1024]{1,0:T(8,128)(2,1)} %bitcast.7, bf16[512,1024]{1,0:T(8,128)(2,1)} %wq.1, bf16[512,1024]{1,0:T(8,128)(2,1)} %get-tuple-element.8.wk, bf16[512,1024]{1,0:T(8,128)(2,1)} %get-tuple-element.7.wv, bf16[1,2048,1024]{2,1,0:T(8,128)(2,1)} %ck_hbm.1, ...), custom_call_target="tpu_custom_call" | custom-call | tf_op jit(solution)/shard_map/attend_block/pallas_call | solution.py:368
  132.0 0.0 all-gather.2.cloned.1.call-done.w_hbm
  132.0 0.0 copy-start
  132.1 0.9 copy-done
  133.0 21.1 %finish.1 = bf16[128,1024]{1,0:T(8,128)(2,1)S(1)} custom-call(bf16[128,1024]{1,0:T(8,128)(2,1)S(1)} %copy-done, bf16[1024,4096]{1,0:T(8,128)(2,1)} %all-gather.2.cloned.1.call-done.w_hbm), custom_call_target="tpu_custom_call" | custom-call | tf_op jit(solution)/shard_map/finish/pallas_call | solution.py:415
  154.1 0.7 copy.18
Async XLA Ops:
  6.5 125.5 %all-gather.2.cloned.1.call-start = ((), (), s32[]{:S(2)}) async-start(), calls=%async_computation | async-start | bytes 9437184 | tf_op jit(solution)/shard_map/all_gather | solution.py:434
  132.0 1.0 copy-start
Sparse Core Ops, SparseCore 0:
  9.2 88.4 all-gather.1

commit v3 on v2

--- a/solution.py
+++ b/solution.py
@@ -35,8 +35,8 @@
 
 
 def block_kernel(
-    ns, nh, nk, tok, wq, wk, wv, ck_hbm, cv_hbm, start_ref, end_ref, out,
-    tokg, wboth, xr, xn, facs, facr, qall, ck, cv, pair, mix, stat, mixs, mixr, statr,
+    ns, nh, nk, tok, wq, wkv, w_out, ck_hbm, cv_hbm, start_ref, end_ref, out,
+    wo, att, attg, town, tsend, tin, got, os, or_, ol, bs, br, ts, tr, vs, vr, tokg, wboth, xr, xn, facs, facr, qall, ck, cv, pair, mix, stat, mixs, mixr, statr,
     zs, zr, ws, wr, wl, fs, fr, gs, gr, qs, qr, cl, ms, mr, ss_, sr_, *rest
 ):
     s, h, k = lax.axis_index("section"), lax.axis_index("head"), lax.axis_index("kv")
@@ -104,8 +104,10 @@
 
     forward(0, tok)
     w_copies, w_locals = [], []
-    for i, w in enumerate((wq, wk, wv)):
-        spot = wboth.at[c, :, pl.ds(i * width, width)]
+    for i, (w, spot) in enumerate((
+        (wq, wboth.at[c, :, pl.ds(0, width)]),
+        (wkv, wboth.at[c, :, pl.ds(width, 2 * width)]),
+    )):
         w_copies.append(send(w, spot, ws.at[i], wr.at[i], core_peer))
         local = pltpu.make_async_copy(w, spot, wl.at[i])
         local.start()
@@ -116,6 +118,9 @@
     ]
     for load in loads:
         load.start()
+    o_copy = send(w_out, wo.at[c], os, or_, core_peer)
+    o_local = pltpu.make_async_copy(w_out, wo.at[c], ol)
+    o_local.start()
 
     own = tok[...].astype(F32)
     squares = jnp.sum(own * own, axis=1, keepdims=True)
@@ -310,17 +315,68 @@
         value = mix[k, :, cols] * factors[0][:, n:n + 1]
         for d in range(nk - 1):
             value = value + mixr[d, :, cols].astype(F32) * factors[d + 1][:, n:n + 1]
-        out[:, cols] = (value / total[:, n:n + 1]).astype(BF16)
+        att[:, cols] = (value / total[:, n:n + 1]).astype(BF16)
+
+    away = [o for o in offsets if o != (0, 0)]
+    b_copies = [
+        send(att, attg.at[i], bs.at[i], br.at[i], plane[o]) for i, o in enumerate(away)
+    ]
+    o_local.wait()
+    o_copy.wait_recv()
+    relays = []
+
+    def relay(piece, i, o, core):
+        index = (2 * at_x(o[0]) + core) * nk + at_k(o[1])
+        target, j = index // per_slot, lax.rem(index, per_slot)
+        here = target == h
+        far = pltpu.make_async_remote_copy(
+            src_ref=piece, dst_ref=got.at[h, j], send_sem=vs.at[i, core], recv_sem=vr.at[h, j],
+            device_id={"head": target}, device_id_type=MESH,
+        )
+        near = pltpu.make_async_copy(piece, got.at[h, j], vr.at[h, j])
+
+        @pl.when(here)
+        def _():
+            near.start()
+
+        @pl.when(jnp.logical_not(here))
+        def _():
+            far.start()
+
+        relays.append((here, far))
+
+    for core in range(2):
+        town[core] = jnp.dot(att[...], wo[core], preferred_element_type=F32).astype(BF16)
+        relay(town.at[core], len(away), (0, 0), core)
+    t_copies = []
+    for i, o in enumerate(away):
+        b_copies[i].wait_recv()
+        back = plane[((nx - o[0]) % nx, (nk - o[1]) % nk)]
+        for core in range(2):
+            tsend[i, core] = jnp.dot(attg[i], wo[core], preferred_element_type=F32).astype(BF16)
+            t_copies.append(send(tsend.at[i, core], tin.at[i, core], ts.at[i, core], tr.at[i, core], back))
+    for i, o in enumerate(away):
+        for core in range(2):
+            t_copies[2 * i + core].wait_recv()
+            relay(tin.at[i, core], i, o, core)
+    for j in range(per_slot):
+        total = None
+        for d in range(nh):
+            origin = lax.rem(h + d, nh)
+            pltpu.make_async_copy(got.at[origin, j], got.at[origin, j], vr.at[origin, j]).wait()
+            part = got[origin, j].astype(F32)
+            total = part if total is None else total + part
+        out[:, j * depth:(j + 1) * depth] = total.astype(BF16)
 
     for copy in pending:
         copy.wait_send()
-    for here, far in forwards:
+    for here, far in forwards + relays:
         @pl.when(jnp.logical_not(here))
         def _():
             far.wait_send()
 
 
-def attend_block(ns, nh, nk, tokens, wq, wk, wv, cache_keys, cache_values, key_start, key_end):
+def attend_block(ns, nh, nk, tokens, wq, wkv, w_out, cache_keys, cache_values, key_start, key_end):
     rows, width = tokens.shape
     depth = wq.shape[0]
     keys = cache_keys.shape[1]
@@ -328,7 +384,19 @@
     group = nx * nk
     more = max(nk - 1, 1)
     dma = pltpu.SemaphoreType.DMA
+    far = group - 1
     scratch = [
+        pltpu.VMEM((2, width, depth), BF16),
+        pltpu.VMEM((rows, width), BF16),
+        pltpu.VMEM((far, rows, width), BF16),
+        pltpu.VMEM((2, rows, depth), BF16),
+        pltpu.VMEM((far, 2, rows, depth), BF16),
+        pltpu.VMEM((far, 2, rows, depth), BF16),
+        pltpu.VMEM((nh, width // depth, rows, depth), BF16),
+        dma, dma, dma,
+        dma((far,)), dma((far,)),
+        dma((far, 2)), dma((far, 2)),
+        dma((group, 2)), dma((nh, width // depth)),
         pltpu.VMEM((nh - 1, rows, width), BF16),
         pltpu.VMEM((2, depth, 3 * width), BF16),
         pltpu.VMEM((group, 2, rows, depth), BF16),
@@ -375,68 +443,14 @@
             collective_id=0, has_side_effects=True, vmem_limit_bytes=60 * 1024 * 1024
         ),
         name="attend_block",
-    )(tokens, wq, wk, wv, cache_keys, cache_values, key_start, key_end)
-
-
-def finish_kernel(nh, attended_ref, w_hbm, out, w, terms, got, wl, os, ors):
-    h = lax.axis_index("head")
-    rows, width = out.shape
-    z_peers = [{"head": lax.rem(h + d, nh)} for d in range(1, nh)]
-    load = pltpu.make_async_copy(w_hbm, w, wl)
-    load.start()
-    greet(z_peers)
-    attended = attended_ref[...]
-    load.wait()
-    copies = []
-    for d in range(1, nh):
-        target = lax.rem(h + d, nh)
-        cols = pl.ds(pl.multiple_of(target * width, width), width)
-        terms[d - 1] = jnp.dot(attended, w[:, cols], preferred_element_type=F32).astype(BF16)
-        copy = pltpu.make_async_remote_copy(
-            src_ref=terms.at[d - 1], dst_ref=got.at[d - 1], send_sem=os.at[d], recv_sem=ors.at[d],
-            device_id=z_peers[d - 1], device_id_type=MESH,
-        )
-        copy.start()
-        copies.append(copy)
-    cols = pl.ds(pl.multiple_of(h * width, width), width)
-    result = jnp.dot(attended, w[:, cols], preferred_element_type=F32)
-    for d, copy in enumerate(copies):
-        copy.wait_recv()
-        result = result + got[d].astype(F32)
-    out[...] = result.astype(BF16)
-    for copy in copies:
-        copy.wait_send()
-
-
-def finish(nh, attended, w_out):
-    rows, width = attended.shape
-    dma = pltpu.SemaphoreType.DMA
-    vmem = pl.BlockSpec(memory_space=pltpu.VMEM)
-    return pl.pallas_call(
-        functools.partial(finish_kernel, nh),
-        out_shape=jax.ShapeDtypeStruct((rows, width), BF16),
-        in_specs=[vmem, pl.BlockSpec(memory_space=pl.ANY)],
-        out_specs=vmem,
-        scratch_shapes=[
-            pltpu.VMEM(w_out.shape, BF16),
-            pltpu.VMEM((max(nh - 1, 1), rows, width), BF16),
-            pltpu.VMEM((max(nh - 1, 1), rows, width), BF16),
-            dma, dma((nh,)), dma((nh,)),
-        ],
-        compiler_params=pltpu.CompilerParams(
-            collective_id=1, has_side_effects=True, vmem_limit_bytes=48 * 1024 * 1024
-        ),
-        name="finish",
-    )(attended, w_out)
+    )(tokens, wq, wkv, w_out, cache_keys, cache_values, key_start, key_end)
 
 
 def shards(ns, nh, nk, tokens, w_query, w_keyvalue, cache_keys, cache_values, key_start, key_end, w_out):
-    w_full = lax.all_gather(w_out, ("section", "kv"), axis=1, tiled=True)
-    attended = attend_block(
-        ns, nh, nk, tokens[0], w_query, w_keyvalue[:, 0, :], w_keyvalue[:, 1, :],
-        cache_keys, cache_values, key_start, key_end,
-    )
-    return finish(nh, attended, w_full)[None]
+    pair_weight = w_keyvalue.reshape(w_keyvalue.shape[0], -1)
+    return attend_block(
+        ns, nh, nk, tokens[0], w_query, pair_weight, w_out, cache_keys, cache_values, key_start, key_end
+    )[None]
 
 
 def solution(mesh):

time: 163 us -> 135 us (0.83)
  between operations: 14.7 us -> 1.31 us
  Pallas kernels: 137 us -> 126 us
  local copies, waits for them, and re-layouts: 9.33 us -> 5.21 us
    pallas_call x1 -> x0, Pallas kernels: 21.1 us -> none  [finish(): pl.pallas_call(functools.partial(finish_kernel, nh), out_shape=jax.ShapeD...]
    pallas_call x1, Pallas kernels: 116 us -> 126 us  [attend_block(): pl.pallas_call(functools.partial(block_kernel, ns, nh, nk), out_shape=jax...]
    slice x1 -> x0, local copies, waits for them, and re-layouts: 5.51 us -> none  [shards(): w_keyvalue[:, 1, :]]
    unnamed x3 -> x2, local copies, waits for them, and re-layouts: 1.65 us -> 5.21 us
    squeeze x1 -> x0, local copies, waits for them, and re-layouts: 2.17 us -> none  [shards(): w_keyvalue[:, 1, :]]
  transfers between devices with their start and end apart: 1 -> 0, of which waited for: 0 -> 0; matrix products, arithmetic and copies ran while one was open for 5% -> 0% of each run, Pallas kernels for 72% -> 0%
where the time goes in v3:
time: 135 us; the launch traced here: 133 us
  Pallas kernels  126 us (93%)
  local copies, waits for them, and re-layouts  5.21 us (4%)
    pallas_call x1, Pallas kernels, attend_block(): pl.pallas_call(functools.partial(block_kernel, ns, nh, nk), out_shape=jax...  126 us
    unnamed x2, local copies, waits for them, and re-layouts  5.21 us

profile of v3, /device:TPU:28, one launch (start us, length us, event | category | flops | bytes accessed | tf_op | source)
XLA Modules:
  0.0 132.9 jit_solution(6081698998816231036)
XLA Ops:
  1.3 3.5 %copy.9 = bf16[64,8,2,1024]{3,1,2,0:T(8,128)(2,1)} copy(bf16[64,8,2,1024]{3,2,1,0:T(2,128)(2,1)} %bitcast.5) | data formatting | bytes 4194304
  4.8 126.4 %attend_block.1 = bf16[128,1024]{1,0:T(8,128)(2,1)} custom-call(bf16[128,1024]{1,0:T(8,128)(2,1)} %bitcast.7, bf16[512,1024]{1,0:T(8,128)(2,1)} %wq.1, bf16[512,2048]{1,0:T(8,128)(2,1)} %bitcast.4, bf16[1024,512]{1,0:T(8,128)(2,1)} %w_out.1, bf16[1,2048,1024]{2,1,0:T(8,128)(2,1)} %ck_hbm.1, bf16[1,2048,1024]{2,1,0:T(8,128)(2,1)} %cv_hbm.1, ...), custom_call_target="tpu_custom_call" | custom-call | tf_op jit(solution)/shard_map/attend_block/pallas_call | solution.py:436
  131.3 1.7 %copy.13 = bf16[1,128,1024]{2,1,0:T(8,128)(2,1)} copy(bf16[1,128,1024]{2,1,0:T(8,128)(2,1)} %bitcast.6) | data formatting | bytes 524288

commit v4 on v3

--- a/solution.py
+++ b/solution.py
@@ -36,8 +36,8 @@
 
 def block_kernel(
     ns, nh, nk, tok, wq, wkv, w_out, ck_hbm, cv_hbm, start_ref, end_ref, out,
-    wo, att, attg, town, tsend, tin, got, os, or_, ol, bs, br, ts, tr, vs, vr, tokg, wboth, xr, xn, facs, facr, qall, ck, cv, pair, mix, stat, mixs, mixr, statr,
-    zs, zr, ws, wr, wl, fs, fr, gs, gr, qs, qr, cl, ms, mr, ss_, sr_, *rest
+    wo, att, attg, town, tsend, tin, got, os, or_, ol, bs, br, ts, tr, vs, vr, tokr, tokl, raw, sqs, sqg, wboth, xr, xn, facs, facr, qall, ck, cv, pair, mix, stat, mixs, mixr, statr,
+    zs, zr, rl, sqss, sqsr, ws, wr, wl, fs, fr, gs, gr, qs, qr, cl, ms, mr, ss_, sr_, *rest
 ):
     s, h, k = lax.axis_index("section"), lax.axis_index("head"), lax.axis_index("kv")
     nx = ns // 2
@@ -71,23 +71,55 @@
         pending.append(copy)
         return copy
 
-    z_copies = [
-        send(tok, tokg.at[d], zs.at[d], zr.at[d], z_peers[d]) for d in range(nh - 1)
+    eye = lax.broadcasted_iota(jnp.int32, (rows, rows), 0) == lax.broadcasted_iota(jnp.int32, (rows, rows), 1)
+
+    def to_row(column):
+        return jnp.sum(jnp.where(eye, jnp.broadcast_to(column, (rows, rows)), 0.0), axis=0, keepdims=True)
+
+    def to_column(row):
+        return jnp.sum(jnp.where(eye, jnp.broadcast_to(row, (rows, rows)), 0.0), axis=1, keepdims=True)
+
+    line = []
+
+    def hop(block, way, t, valid):
+        store, peer, inside = (tokr, h + 1, h + 1 < nh) if way == 0 else (tokl, h - 1, h >= 1)
+        go = valid & inside
+        copy = pltpu.make_async_remote_copy(
+            src_ref=block, dst_ref=store.at[t], send_sem=zs.at[way, t], recv_sem=zr.at[way, t],
+            device_id={"head": lax.rem(peer + nh, nh)}, device_id_type=MESH,
+        )
+
+        @pl.when(go)
+        def _():
+            copy.start()
+
+        line.append((go, copy))
+
+    always = h >= 0
+    raw_load = pltpu.make_async_copy(wkv, raw, rl)
+    raw_load.start()
+    hop(tok, 0, 0, always)
+    hop(tok, 1, 0, always)
+    own = tok[...].astype(F32)
+    sqs[...] = jnp.broadcast_to(to_row(jnp.sum(own * own, axis=1, keepdims=True)), sqs.shape)
+    sq_copies = [
+        send(sqs, sqg.at[d], sqss.at[d], sqsr.at[d], z_peers[d]) for d in range(nh - 1)
     ]
 
     forwards = []
 
-    def forward(d, block):
-        origin = lax.rem(h + nh - d, nh)
+    def forward(slot, block, origin, valid):
         for j in range(per_slot):
             index = origin * per_slot + j
             section, kv = index // nk, lax.rem(index, nk)
             core = lax.rem(section, 2)
             src = block.at[:, pl.ds(j * depth, depth)]
             dst = xr.at[mine, core]
-            here = (section // 2 == x) & (kv == k)
+            here = valid & (section // 2 == x) & (kv == k)
+            leave = valid & jnp.logical_not((section // 2 == x) & (kv == k))
+            section = lax.rem(section, ns)
             far = pltpu.make_async_remote_copy(
-                src_ref=src, dst_ref=dst, send_sem=gs.at[d, j], recv_sem=gr.at[mine, core],
+                src_ref=src, dst_ref=dst, send_sem=gs.at[slot, j], recv_sem=gr.at[mine, core],
                 device_id={"section": (section // 2) * 2 + c, "kv": kv}, device_id_type=MESH,
             )
             near = pltpu.make_async_copy(src, dst, gr.at[mine, core])
@@ -96,22 +128,17 @@
             def _():
                 near.start()
 
-            @pl.when(jnp.logical_not(here))
+            @pl.when(leave)
             def _():
                 far.start()
 
-            forwards.append((here, far))
-
-    forward(0, tok)
-    w_copies, w_locals = [], []
-    for i, (w, spot) in enumerate((
-        (wq, wboth.at[c, :, pl.ds(0, width)]),
-        (wkv, wboth.at[c, :, pl.ds(width, 2 * width)]),
-    )):
-        w_copies.append(send(w, spot, ws.at[i], wr.at[i], core_peer))
-        local = pltpu.make_async_copy(w, spot, wl.at[i])
-        local.start()
-        w_locals.append(local)
+            forwards.append((leave, far))
+
+    forward(0, tok, h, always)
+    spot = wboth.at[c, :, pl.ds(0, width)]
+    w_copies = [send(wq, spot, ws.at[0], wr.at[0], core_peer)]
+    w_local = pltpu.make_async_copy(wq, spot, wl)
+    w_local.start()
     loads = [
         pltpu.make_async_copy(ck_hbm.at[0], ck, cl.at[0]),
         pltpu.make_async_copy(cv_hbm.at[0], cv, cl.at[1]),
@@ -122,33 +149,43 @@
     o_local = pltpu.make_async_copy(w_out, wo.at[c], ol)
     o_local.start()
 
-    own = tok[...].astype(F32)
-    squares = jnp.sum(own * own, axis=1, keepdims=True)
+    squares = sqs[:1]
     for d in range(1, nh):
-        z_copies[d - 1].wait_recv()
-        forward(d, tokg.at[d - 1])
-        part = tokg[d - 1].astype(F32)
-        squares = squares + jnp.sum(part * part, axis=1, keepdims=True)
-    factor = lax.rsqrt(squares * (1.0 / (width * nh)) + 1e-05)
-    facs[...] = jnp.broadcast_to(factor, (rows, HD))
+        sq_copies[d - 1].wait_recv()
+        squares = squares + sqg[d - 1][:1]
+    facs[...] = jnp.broadcast_to(lax.rsqrt(squares * (1.0 / (width * nh)) + 1e-05), facs.shape)
     facr[mine] = facs[...]
     f_copies = []
     for i, o in enumerate(offsets):
         if o != (0, 0):
             f_copies.append(send(facs, facr.at[mine], fs.at[i], fr.at[i], plane[o]))
-    for copy in w_copies:
-        copy.wait_recv()
-    for copy in w_locals:
-        copy.wait()
-    for g in range(nx * nk):
-        for core in range(2):
-            pltpu.make_async_copy(xr.at[g, core], xr.at[g, core], gr.at[g, core]).wait()
+    for t in range(nh - 1):
+        for way, store, origin, valid in (
+            (0, tokr, h - t - 1, h >= t + 1), (1, tokl, h + t + 1, h + t + 1 < nh)
+        ):
+            @pl.when(valid)
+            def _():
+                pltpu.make_async_copy(store.at[t], store.at[t], zr.at[way, t]).wait()
+
+            if t + 1 < nh - 1:
+                hop(store.at[t], way, t + 1, valid)
+            forward(1 + 2 * t + way, store.at[t], lax.rem(origin + nh, nh), valid)
+        if t == 0:
+            raw_load.wait()
+            for i in range(2):
+                wboth[c, :, (1 + i) * width:(2 + i) * width] = raw[:, i, :]
+            spot = wboth.at[c, :, pl.ds(width, 2 * width)]
+            w_copies.append(send(spot, spot, ws.at[1], wr.at[1], core_peer))
     for copy in f_copies:
         copy.wait_recv()
     for g in range(nx * nk):
-        scale = facr[g][:, :1]
+        scale = to_column(facr[g][:1])
         for core in range(2):
+            pltpu.make_async_copy(xr.at[g, core], xr.at[g, core], gr.at[g, core]).wait()
             xn[core, pl.ds(g * rows, rows), :] = (xr[g, core].astype(F32) * scale).astype(BF16)
+    for copy in w_copies:
+        copy.wait_recv()
+    w_local.wait()
 
     parts = split_parts(width)
     per = len(rest) // len(parts)
@@ -214,13 +251,13 @@
     multiply(3)
     sum_a = second_hop(0, hop_a)
     sum_b = second_hop(1, hop_b)
+    hop_k = first_hop(2)
+    hop_v = first_hop(3)
     qall[k, :, :half] = last(0, *sum_a)
     qall[k, :, half:] = last(1, *sum_b)
     q_copies = [
         send(qall.at[k], qall.at[k], qs.at[d], qr.at[d], plane[(0, d)]) for d in range(1, nk)
     ]
-    hop_k = first_hop(2)
-    hop_v = first_hop(3)
     for load in loads:
         load.wait()
 
@@ -370,7 +407,12 @@
 
     for copy in pending:
         copy.wait_send()
-    for here, far in forwards + relays:
+    for gone, copy in forwards + line:
+        @pl.when(gone)
+        def _():
+            copy.wait_send()
+
+    for here, far in relays:
         @pl.when(jnp.logical_not(here))
         def _():
             far.wait_send()
@@ -398,11 +440,15 @@
         dma((far, 2)), dma((far, 2)),
         dma((group, 2)), dma((nh, width // depth)),
         pltpu.VMEM((nh - 1, rows, width), BF16),
+        pltpu.VMEM((nh - 1, rows, width), BF16),
+        pltpu.VMEM(wkv.shape, BF16),
+        pltpu.VMEM((8, rows), F32),
+        pltpu.VMEM((nh - 1, 8, rows), F32),
         pltpu.VMEM((2, depth, 3 * width), BF16),
         pltpu.VMEM((group, 2, rows, depth), BF16),
         pltpu.VMEM((2, group * rows, depth), BF16),
-        pltpu.VMEM((rows, HD), F32),
-        pltpu.VMEM((group, rows, HD), F32),
+        pltpu.VMEM((8, rows), F32),
+        pltpu.VMEM((group, 8, rows), F32),
         pltpu.VMEM((nk, rows, width), BF16),
         pltpu.VMEM((keys, width), BF16),
         pltpu.VMEM((keys, width), BF16),
@@ -412,10 +458,11 @@
         pltpu.VMEM((more, rows, width), BF16),
         pltpu.VMEM((more, rows, width), BF16),
         pltpu.VMEM((more, rows, HD), F32),
+        dma((2, nh - 1)), dma((2, nh - 1)), dma,
         dma((nh - 1,)), dma((nh - 1,)),
-        dma((3,)), dma((3,)), dma((3,)),
+        dma((2,)), dma((2,)), dma,
         dma((group,)), dma((group,)),
-        dma((nh, width // depth)), dma((group, 2)),
+        dma((2 * nh - 1, width // depth)), dma((group, 2)),
         dma((nk,)), dma((nk,)),
         dma((2,)),
         dma((nk,)), dma((nk,)), dma((nk,)), dma((nk,)),
@@ -447,9 +494,8 @@
 
 
 def shards(ns, nh, nk, tokens, w_query, w_keyvalue, cache_keys, cache_values, key_start, key_end, w_out):
-    pair_weight = w_keyvalue.reshape(w_keyvalue.shape[0], -1)
     return attend_block(
-        ns, nh, nk, tokens[0], w_query, pair_weight, w_out, cache_keys, cache_values, key_start, key_end
+        ns, nh, nk, tokens[0], w_query, w_keyvalue, w_out, cache_keys, cache_values, key_start, key_end
     )[None]
 
 

time: 135 us -> 127 us (0.941); the launches traced: 133 us -> 127 us
  local copies, waits for them, and re-layouts: 5.21 us -> 1.67 us
  Pallas kernels: 126 us -> 124 us
    unnamed x2 -> x1, local copies, waits for them, and re-layouts: 5.21 us -> 1.67 us
    pallas_call x1, Pallas kernels: 126 us -> 124 us  [attend_block(): pl.pallas_call(functools.partial(block_kernel, ns, nh, nk), out_shape=jax...]
where the time goes in v4:
time: 127 us
  Pallas kernels  124 us (98%)
  local copies, waits for them, and re-layouts  1.67 us (1%)
  between operations  1.31 us (1%)
    pallas_call x1, Pallas kernels, attend_block(): pl.pallas_call(functools.partial(block_kernel, ns, nh, nk), out_shape=jax...  124 us

profile of v4, /device:TPU:28, one launch (start us, length us, event | category | flops | bytes accessed | tf_op | source)
XLA Modules:
  0.0 126.6 jit_solution(1618553026759489956)
XLA Ops:
  1.3 123.7 %attend_block.1 = bf16[128,1024]{1,0:T(8,128)(2,1)} custom-call(bf16[128,1024]{1,0:T(8,128)(2,1)} %bitcast.3, bf16[512,1024]{1,0:T(8,128)(2,1)} %wq.1, bf16[512,2,1024]{2,1,0:T(2,128)(2,1)} %wkv.1, bf16[1024,512]{1,0:T(8,128)(2,1)} %w_out.1, bf16[1,2048,1024]{2,1,0:T(8,128)(2,1)} %ck_hbm.1, bf16[1,2048,1024]{2,1,0:T(8,128)(2,1)} %cv_hbm.1, ...), custom_call_target="tpu_custom_call" | custom-call | tf_op jit(solution)/shard_map/attend_block/pallas_call | solution.py:483
  125.0 1.7 %copy.12 = bf16[1,128,1024]{2,1,0:T(8,128)(2,1)} copy(bf16[1,128,1024]{2,1,0:T(8,128)(2,1)} %bitcast.2) | data formatting | bytes 524288

commit v5 on v4

--- a/solution.py
+++ b/solution.py
@@ -81,11 +81,12 @@
 
     line = []
 
-    def hop(block, way, t, valid):
+    def hop(block, way, t, j, valid):
         store, peer, inside = (tokr, h + 1, h + 1 < nh) if way == 0 else (tokl, h - 1, h >= 1)
         go = valid & inside
         copy = pltpu.make_async_remote_copy(
-            src_ref=block, dst_ref=store.at[t], send_sem=zs.at[way, t], recv_sem=zr.at[way, t],
+            src_ref=block.at[:, pl.ds(j * depth, depth)], dst_ref=store.at[t, :, pl.ds(j * depth, depth)],
+            send_sem=zs.at[way, t, j], recv_sem=zr.at[way, t, j],
             device_id={"head": lax.rem(peer + nh, nh)}, device_id_type=MESH,
         )
 
@@ -98,8 +99,9 @@
     always = h >= 0
     raw_load = pltpu.make_async_copy(wkv, raw, rl)
     raw_load.start()
-    hop(tok, 0, 0, always)
-    hop(tok, 1, 0, always)
+    for j in range(per_slot):
+        hop(tok, 0, 0, j, always)
+        hop(tok, 1, 0, j, always)
     own = tok[...].astype(F32)
     sqs[...] = jnp.broadcast_to(to_row(jnp.sum(own * own, axis=1, keepdims=True)), sqs.shape)
     sq_copies = [
@@ -108,8 +110,8 @@
 
     forwards = []
 
-    def forward(slot, block, origin, valid):
-        for j in range(per_slot):
+    def forward(slot, block, origin, pieces, valid):
+        for j in pieces:
             index = origin * per_slot + j
             section, kv = index // nk, lax.rem(index, nk)
             core = lax.rem(section, 2)
@@ -134,7 +136,7 @@
 
             forwards.append((leave, far))
 
-    forward(0, tok, h, always)
+    forward(0, tok, h, range(per_slot), always)
     spot = wboth.at[c, :, pl.ds(0, width)]
     w_copies = [send(wq, spot, ws.at[0], wr.at[0], core_peer)]
     w_local = pltpu.make_async_copy(wq, spot, wl)
@@ -160,16 +162,19 @@
         if o != (0, 0):
             f_copies.append(send(facs, facr.at[mine], fs.at[i], fr.at[i], plane[o]))
     for t in range(nh - 1):
-        for way, store, origin, valid in (
-            (0, tokr, h - t - 1, h >= t + 1), (1, tokl, h + t + 1, h + t + 1 < nh)
-        ):
-            @pl.when(valid)
-            def _():
-                pltpu.make_async_copy(store.at[t], store.at[t], zr.at[way, t]).wait()
-
-            if t + 1 < nh - 1:
-                hop(store.at[t], way, t + 1, valid)
-            forward(1 + 2 * t + way, store.at[t], lax.rem(origin + nh, nh), valid)
+        for j in range(per_slot):
+            for way, store, origin, valid in (
+                (0, tokr, h - t - 1, h >= t + 1), (1, tokl, h + t + 1, h + t + 1 < nh)
+            ):
+                piece = store.at[t, :, pl.ds(j * depth, depth)]
+
+                @pl.when(valid)
+                def _():
+                    pltpu.make_async_copy(piece, piece, zr.at[way, t, j]).wait()
+
+                if t + 1 < nh - 1:
+                    hop(store.at[t], way, t + 1, j, valid)
+                forward(1 + 2 * t + way, store.at[t], lax.rem(origin + nh, nh), (j,), valid)
         if t == 0:
             raw_load.wait()
             for i in range(2):
@@ -267,17 +272,29 @@
     lane = lax.broadcasted_iota(jnp.int32, (rows, HD), 1)
 
     def resident(block, begin, end):
-        @pl.loop(begin, end)
-        def _(n):
-            cols = pl.ds(pl.multiple_of(n * HD, HD), HD)
-            scores = lax.dot_general(
-                qall[block, :, cols], ck[:, cols], contract, preferred_element_type=F32
-            ) + bias
-            peak = jnp.maximum(jnp.max(scores, axis=1, keepdims=True), FLOOR)
-            weights = jnp.exp2((scores - peak) * RATE).astype(BF16)
-            total = jnp.sum(weights.astype(F32), axis=1, keepdims=True)
-            mix[block, :, cols] = jnp.dot(weights, cv[:, cols], preferred_element_type=F32)
-            stat[block] = jnp.where(lane == n, peak, jnp.where(lane == n + HD // 2, total, stat[block]))
+        together = 2 if (end - begin) % 2 == 0 else 1
+
+        @pl.loop(0, (end - begin) // together)
+        def _(step):
+            first = begin + step * together
+            columns = [
+                pl.ds(pl.multiple_of((first + m) * HD, HD), HD) for m in range(together)
+            ]
+            scores = [
+                lax.dot_general(
+                    qall[block, :, cols], ck[:, cols], contract, preferred_element_type=F32
+                ) + bias
+                for cols in columns
+            ]
+            peaks = [jnp.maximum(jnp.max(each, axis=1, keepdims=True), FLOOR) for each in scores]
+            stats = stat[block]
+            for m, cols in enumerate(columns):
+                weights = jnp.exp2((scores[m] - peaks[m]) * RATE).astype(BF16)
+                total = jnp.sum(weights.astype(F32), axis=1, keepdims=True)
+                mix[block, :, cols] = jnp.dot(weights, cv[:, cols], preferred_element_type=F32)
+                n = first + m
+                stats = jnp.where(lane == n, peaks[m], jnp.where(lane == n + HD // 2, total, stats))
+            stat[block] = stats
 
     def fresh(block, target):
         query_place = block * rows + lax.broadcasted_iota(jnp.int32, (rows, rows), 0)
@@ -322,12 +339,17 @@
         resident(at_k(nk - 1), heads // 2, heads)
     pair[:, :width] = last(2, *sum_k)
     pair[:, width:] = last(3, *sum_v)
-    arrivals = []
+    part_rows = rows // 2
+    spans = [pl.ds(r * part_rows, part_rows) for r in range(2)]
+    arrivals, mix_copies = [], []
     for d in range(1, nk):
         other = at_k(d)
         fresh(other, mixs.at[d - 1])
         arrivals.append(send(stat.at[other], statr.at[d - 1], ss_.at[d], sr_.at[d], plane[(0, d)]))
-        arrivals.append(send(mixs.at[d - 1], mixr.at[d - 1], ms.at[d], mr.at[d], plane[(0, d)]))
+        for r, span in enumerate(spans):
+            mix_copies.append(send(
+                mixs.at[d - 1, span], mixr.at[d - 1, span], ms.at[d, r], mr.at[d, r], plane[(0, d)]
+            ))
     fresh(k, None)
     for copy in arrivals:
         copy.wait_recv()
@@ -347,30 +369,34 @@
     for d in range(nk - 1):
         factors.append(jnp.exp2((tops(statr[d]) - highest) * RATE))
         total = total + sums(statr[d]) * factors[-1]
-    for n in range(heads):
-        cols = pl.ds(n * HD, HD)
-        value = mix[k, :, cols] * factors[0][:, n:n + 1]
+    away = [o for o in offsets if o != (0, 0)]
+    b_copies = []
+    for r, span in enumerate(spans):
         for d in range(nk - 1):
-            value = value + mixr[d, :, cols].astype(F32) * factors[d + 1][:, n:n + 1]
-        att[:, cols] = (value / total[:, n:n + 1]).astype(BF16)
-
-    away = [o for o in offsets if o != (0, 0)]
-    b_copies = [
-        send(att, attg.at[i], bs.at[i], br.at[i], plane[o]) for i, o in enumerate(away)
-    ]
+            mix_copies[2 * d + r].wait_recv()
+        low, high = r * part_rows, (r + 1) * part_rows
+        for n in range(heads):
+            cols = pl.ds(n * HD, HD)
+            value = mix[k, span, cols] * factors[0][low:high, n:n + 1]
+            for d in range(nk - 1):
+                value = value + mixr[d, span, cols].astype(F32) * factors[d + 1][low:high, n:n + 1]
+            att[span, cols] = (value / total[low:high, n:n + 1]).astype(BF16)
+        b_copies.append([
+            send(att.at[span], attg.at[i, span], bs.at[i, r], br.at[i, r], plane[o]) for i, o in enumerate(away)
+        ])
     o_local.wait()
     o_copy.wait_recv()
     relays = []
 
-    def relay(piece, i, o, core):
+    def relay(piece, i, o, core, r):
         index = (2 * at_x(o[0]) + core) * nk + at_k(o[1])
         target, j = index // per_slot, lax.rem(index, per_slot)
         here = target == h
         far = pltpu.make_async_remote_copy(
-            src_ref=piece, dst_ref=got.at[h, j], send_sem=vs.at[i, core], recv_sem=vr.at[h, j],
+            src_ref=piece, dst_ref=got.at[h, j, r], send_sem=vs.at[i, core, r], recv_sem=vr.at[h, j, r],
             device_id={"head": target}, device_id_type=MESH,
         )
-        near = pltpu.make_async_copy(piece, got.at[h, j], vr.at[h, j])
+        near = pltpu.make_async_copy(piece, got.at[h, j, r], vr.at[h, j, r])
 
         @pl.when(here)
         def _():
@@ -382,28 +408,34 @@
 
         relays.append((here, far))
 
-    for core in range(2):
-        town[core] = jnp.dot(att[...], wo[core], preferred_element_type=F32).astype(BF16)
-        relay(town.at[core], len(away), (0, 0), core)
-    t_copies = []
-    for i, o in enumerate(away):
-        b_copies[i].wait_recv()
-        back = plane[((nx - o[0]) % nx, (nk - o[1]) % nk)]
+    for r, span in enumerate(spans):
         for core in range(2):
-            tsend[i, core] = jnp.dot(attg[i], wo[core], preferred_element_type=F32).astype(BF16)
-            t_copies.append(send(tsend.at[i, core], tin.at[i, core], ts.at[i, core], tr.at[i, core], back))
-    for i, o in enumerate(away):
-        for core in range(2):
-            t_copies[2 * i + core].wait_recv()
-            relay(tin.at[i, core], i, o, core)
-    for j in range(per_slot):
-        total = None
-        for d in range(nh):
-            origin = lax.rem(h + d, nh)
-            pltpu.make_async_copy(got.at[origin, j], got.at[origin, j], vr.at[origin, j]).wait()
-            part = got[origin, j].astype(F32)
-            total = part if total is None else total + part
-        out[:, j * depth:(j + 1) * depth] = total.astype(BF16)
+            town[core, span] = jnp.dot(att[span], wo[core], preferred_element_type=F32).astype(BF16)
+            relay(town.at[core, span], len(away), (0, 0), core, r)
+    t_copies = {}
+    for r, span in enumerate(spans):
+        for i, o in enumerate(away):
+            b_copies[r][i].wait_recv()
+            back = plane[((nx - o[0]) % nx, (nk - o[1]) % nk)]
+            for core in range(2):
+                tsend[i, core, span] = jnp.dot(attg[i, span], wo[core], preferred_element_type=F32).astype(BF16)
+                t_copies[r, i, core] = send(
+                    tsend.at[i, core, span], tin.at[i, core, span], ts.at[i, core, r], tr.at[i, core, r], back
+                )
+    for r, span in enumerate(spans):
+        for i, o in enumerate(away):
+            for core in range(2):
+                t_copies[r, i, core].wait_recv()
+                relay(tin.at[i, core, span], i, o, core, r)
+    for r, span in enumerate(spans):
+        for j in range(per_slot):
+            total = None
+            for d in range(nh):
+                origin = lax.rem(h + d, nh)
+                pltpu.make_async_copy(got.at[origin, j, r], got.at[origin, j, r], vr.at[origin, j, r]).wait()
+                part = got[origin, j, r].astype(F32)
+                total = part if total is None else total + part
+            out[span, j * depth:(j + 1) * depth] = total.astype(BF16)
 
     for copy in pending:
         copy.wait_send()
@@ -434,11 +466,11 @@
         pltpu.VMEM((2, rows, depth), BF16),
         pltpu.VMEM((far, 2, rows, depth), BF16),
         pltpu.VMEM((far, 2, rows, depth), BF16),
-        pltpu.VMEM((nh, width // depth, rows, depth), BF16),
+        pltpu.VMEM((nh, width // depth, 2, rows // 2, depth), BF16),
         dma, dma, dma,
-        dma((far,)), dma((far,)),
         dma((far, 2)), dma((far, 2)),
-        dma((group, 2)), dma((nh, width // depth)),
+        dma((far, 2, 2)), dma((far, 2, 2)),
+        dma((group, 2, 2)), dma((nh, width // depth, 2)),
         pltpu.VMEM((nh - 1, rows, width), BF16),
         pltpu.VMEM((nh - 1, rows, width), BF16),
         pltpu.VMEM(wkv.shape, BF16),
@@ -458,14 +490,14 @@
         pltpu.VMEM((more, rows, width), BF16),
         pltpu.VMEM((more, rows, width), BF16),
         pltpu.VMEM((more, rows, HD), F32),
-        dma((2, nh - 1)), dma((2, nh - 1)), dma,
+        dma((2, nh - 1, width // depth)), dma((2, nh - 1, width // depth)), dma,
         dma((nh - 1,)), dma((nh - 1,)),
         dma((2,)), dma((2,)), dma,
         dma((group,)), dma((group,)),
         dma((2 * nh - 1, width // depth)), dma((group, 2)),
         dma((nk,)), dma((nk,)),
         dma((2,)),
-        dma((nk,)), dma((nk,)), dma((nk,)), dma((nk,)),
+        dma((nk, 2)), dma((nk, 2)), dma((nk,)), dma((nk,)),
     ]
     for start, cols, x_first, kind in split_parts(width):
         n1, n2 = (nx, nk) if x_first else (nk, nx)

time: 127 us -> 126 us (level)
  Pallas kernels: 124 us -> 122 us
    pallas_call x1, Pallas kernels: 124 us -> 122 us  [attend_block(): pl.pallas_call(functools.partial(block_kernel, ns, nh, nk), out_shape=jax...]
where the time goes in v5:
time: 126 us; the launch traced here: 125 us
  Pallas kernels  122 us (97%)
  local copies, waits for them, and re-layouts  1.67 us (1%)
  between operations  1.31 us (1%)
    pallas_call x1, Pallas kernels, attend_block(): pl.pallas_call(functools.partial(block_kernel, ns, nh, nk), out_shape=jax...  122 us

profile of v5, /device:TPU:28, one launch (start us, length us, event | category | flops | bytes accessed | tf_op | source)
XLA Modules:
  0.0 124.7 jit_solution(3015497829994530352)
XLA Ops:
  1.3 121.7 %attend_block.1 = bf16[128,1024]{1,0:T(8,128)(2,1)} custom-call(bf16[128,1024]{1,0:T(8,128)(2,1)} %bitcast.3, bf16[512,1024]{1,0:T(8,128)(2,1)} %wq.1, bf16[512,2,1024]{2,1,0:T(2,128)(2,1)} %wkv.1, bf16[1024,512]{1,0:T(8,128)(2,1)} %w_out.1, bf16[1,2048,1024]{2,1,0:T(8,128)(2,1)} %ck_hbm.1, bf16[1,2048,1024]{2,1,0:T(8,128)(2,1)} %cv_hbm.1, ...), custom_call_target="tpu_custom_call" | custom-call | tf_op jit(solution)/shard_map/attend_block/pallas_call | solution.py:515
  123.0 1.7 %copy.12 = bf16[1,128,1024]{2,1,0:T(8,128)(2,1)} copy(bf16[1,128,1024]{2,1,0:T(8,128)(2,1)} %bitcast.2) | data formatting | bytes 524288

commit v6 on v5

--- a/solution.py
+++ b/solution.py
@@ -302,27 +302,35 @@
         usable = new_place <= query_place
         stats = stat[block]
         merged = stats
+        spots = [pl.ds(n * HD, HD) for n in range(heads)]
+        scores = [
+            jnp.where(
+                usable,
+                lax.dot_general(qall[block, :, cols], pair[:, cols], contract, preferred_element_type=F32),
+                LOW,
+            )
+            for cols in spots
+        ]
+        weights, shrinks = [], []
         for n in range(heads):
-            cols = pl.ds(n * HD, HD)
-            scores = lax.dot_general(
-                qall[block, :, cols], pair[:, cols], contract, preferred_element_type=F32
+            before = stats[:, n:n + 1]
+            peak = jnp.maximum(before, jnp.max(scores[n], axis=1, keepdims=True))
+            weights.append(jnp.exp2((scores[n] - peak) * RATE).astype(BF16))
+            shrinks.append(jnp.exp2((before - peak) * RATE))
+            total = stats[:, n + HD // 2:n + HD // 2 + 1] * shrinks[n] + jnp.sum(
+                weights[n].astype(F32), axis=1, keepdims=True
             )
-            scores = jnp.where(usable, scores, LOW)
-            before = stats[:, n:n + 1]
-            peak = jnp.maximum(before, jnp.max(scores, axis=1, keepdims=True))
-            weights = jnp.exp2((scores - peak) * RATE).astype(BF16)
-            shrink = jnp.exp2((before - peak) * RATE)
-            total = stats[:, n + HD // 2:n + HD // 2 + 1] * shrink + jnp.sum(
-                weights.astype(F32), axis=1, keepdims=True
-            )
-            value = mix[block, :, cols] * shrink + jnp.dot(
-                weights, pair[:, pl.ds(width + n * HD, HD)], preferred_element_type=F32
-            )
+            merged = jnp.where(lane == n, peak, jnp.where(lane == n + HD // 2, total, merged))
+        products = [
+            jnp.dot(weights[n], pair[:, pl.ds(width + n * HD, HD)], preferred_element_type=F32)
+            for n in range(heads)
+        ]
+        for n, cols in enumerate(spots):
+            value = mix[block, :, cols] * shrinks[n] + products[n]
             if target is None:
                 mix[block, :, cols] = value
             else:
                 target[:, cols] = value.astype(BF16)
-            merged = jnp.where(lane == n, peak, jnp.where(lane == n + HD // 2, total, merged))
         stat[block] = merged
 
     stat[...] = jnp.zeros_like(stat)

time: 126 us -> 126 us (level)
  no operation moved by 1% of the time
where the time goes in v6:
time: 126 us; the launch traced here: 124 us
  Pallas kernels  121 us (96%)
  local copies, waits for them, and re-layouts  1.67 us (1%)
  between operations  1.31 us (1%)
    pallas_call x1, Pallas kernels, attend_block(): pl.pallas_call(functools.partial(block_kernel, ns, nh, nk), out_shape=jax...  121 us

profile of v6, /device:TPU:28, one launch (start us, length us, event | category | flops | bytes accessed | tf_op | source)
XLA Modules:
  0.0 124.3 jit_solution(1806205689925780372)
XLA Ops:
  1.3 121.3 %attend_block.1 = bf16[128,1024]{1,0:T(8,128)(2,1)} custom-call(bf16[128,1024]{1,0:T(8,128)(2,1)} %bitcast.3, bf16[512,1024]{1,0:T(8,128)(2,1)} %wq.1, bf16[512,2,1024]{2,1,0:T(2,128)(2,1)} %wkv.1, bf16[1024,512]{1,0:T(8,128)(2,1)} %w_out.1, bf16[1,2048,1024]{2,1,0:T(8,128)(2,1)} %ck_hbm.1, bf16[1,2048,1024]{2,1,0:T(8,128)(2,1)} %cv_hbm.1, ...), custom_call_target="tpu_custom_call" | custom-call | tf_op jit(solution)/shard_map/attend_block/pallas_call | solution.py:523
  122.6 1.7 %copy.12 = bf16[1,128,1024]{2,1,0:T(8,128)(2,1)} copy(bf16[1,128,1024]{2,1,0:T(8,128)(2,1)} %bitcast.2) | data formatting | bytes 524288
